TPU v7x, 512 devices: a whole 4x8x8 slice. The times are simulated.
512 devices in a mesh: wide: 64 (over z, x, core), narrow: 8 (over y).
Axes of the slice: x: 4, y: 8, z: 8, core: 2. Of those that a mesh axis runs over, the one named last changes fastest.
Arguments:
- encodings: bfloat16 [128, 128, 768], P('wide', 'narrow'), may hold values from -6 to 6
- image_slot: int32 [128], replicated, may hold values from 0 to 127, as said below
- pairs: int32 [512, 2], replicated, may hold values from 0 to 127, as said below
- attn_weights: bfloat16 [4, 768, 768], P(None, 'wide'), may hold values from -0.21875 to 0.21875
- head_scale: float32 [12], replicated, may hold values from 2 to 12
- cotangent: bfloat16 [512, 2, 128, 768], P(('wide', 'narrow')), may hold values from -6 to 6
Outputs:
- decoded: bfloat16 [512, 2, 128, 768], P(('wide', 'narrow'))
- encoding_gradient: bfloat16 [128, 128, 768], P('wide', 'narrow')
Inputs may be any that keep to these rules, and one draw needn't show every extreme that they name: A permutation of the 128 storage rows; image a is stored at row image_slot[a], owned by index image_slot[a] // 2 of wide. In each aligned block of 8 pairs, the 16 images named have pairwise different owners (the owner of image a being image_slot[a] // 2).
All inputs are finite; a program needn't handle non-finite values.
Results may differ from a plain program's by a relative error of at most 0.0062.
Values may be sent and summed in bfloat16 or wider, within the bound.
A program may use at most 64 MiB of HBM per device.

v0:
```python
import jax
import jax.numpy as jnp
from jax import lax
from jax.sharding import PartitionSpec as P


def dot_transposed(left, right):
    return lax.dot_general(
        left, right, (((1,), (1,)), ((), ())), preferred_element_type=jnp.float32
    )


def head_norm(projected, sides, tokens, head_count, head_dim):
    per_head = projected.reshape(sides, tokens, head_count, head_dim)
    inv_scale = lax.rsqrt(jnp.mean(per_head * per_head, axis=-1, keepdims=True) + 1e-06)
    return (per_head * inv_scale, inv_scale)


def head_back(upstream, normed, inv_scale, rows, features):
    result = (upstream - normed * jnp.mean(upstream * normed, axis=-1, keepdims=True)) * inv_scale
    return result.astype(jnp.bfloat16).reshape(rows, features)


def pair_pass(pair_views, cot_view, weights, head_scale):
    sides, tokens, features = pair_views.shape
    head_count = head_scale.shape[0]
    head_dim = features // head_count
    rows = sides * tokens
    flat_views = pair_views.reshape(rows, features)
    context_f = pair_views[::-1].astype(jnp.float32)
    centred = context_f - jnp.mean(context_f, axis=-1, keepdims=True)
    inv_std = lax.rsqrt(jnp.mean(centred * centred, axis=-1, keepdims=True) + 1e-06)
    y_hat = centred * inv_std
    y_norm = y_hat.astype(jnp.bfloat16).reshape(rows, features)
    query_proj = jnp.dot(flat_views, weights[0], preferred_element_type=jnp.float32)
    key_proj = jnp.dot(y_norm, weights[1], preferred_element_type=jnp.float32)
    value_proj = jnp.dot(y_norm, weights[2], preferred_element_type=jnp.float32)
    query_unit, query_scale = head_norm(query_proj, sides, tokens, head_count, head_dim)
    key_unit, key_scale = head_norm(key_proj, sides, tokens, head_count, head_dim)
    query_round = query_unit.astype(jnp.bfloat16)
    key_round = key_unit.astype(jnp.bfloat16)
    value_round = value_proj.astype(jnp.bfloat16).reshape(sides, tokens, head_count, head_dim)
    factor = (head_scale / head_dim)[None, :, None, None]
    scores = (
        jnp.einsum("sqhd,skhd->shqk", query_round, key_round, preferred_element_type=jnp.float32)
        * factor
    )
    exponent = jnp.exp(scores)
    softmax_probs = exponent / jnp.sum(exponent, axis=-1, keepdims=True)
    prob_round = softmax_probs.astype(jnp.bfloat16)
    attended = jnp.einsum(
        "shqk,skhd->sqhd", prob_round, value_round, preferred_element_type=jnp.float32
    )
    attended = attended.astype(jnp.bfloat16).reshape(rows, features)
    decoded = (
        flat_views.astype(jnp.float32)
        + jnp.dot(attended, weights[3], preferred_element_type=jnp.float32)
    ).astype(jnp.bfloat16)
    cot_flat = cot_view.reshape(rows, features)
    attn_grad = (
        dot_transposed(cot_flat, weights[3])
        .astype(jnp.bfloat16)
        .reshape(sides, tokens, head_count, head_dim)
    )
    prob_grad = jnp.einsum(
        "sqhd,skhd->shqk", attn_grad, value_round, preferred_element_type=jnp.float32
    )
    score_grad = (
        softmax_probs
        * (prob_grad - jnp.sum(softmax_probs * prob_grad, axis=-1, keepdims=True))
        * factor
    )
    score_grad = score_grad.astype(jnp.bfloat16)
    value_gradient = jnp.einsum(
        "shqk,sqhd->skhd", prob_round, attn_grad, preferred_element_type=jnp.float32
    )
    value_gradient = value_gradient.astype(jnp.bfloat16).reshape(rows, features)
    query_back = jnp.einsum(
        "shqk,skhd->sqhd", score_grad, key_round, preferred_element_type=jnp.float32
    )
    key_back = jnp.einsum(
        "shqk,sqhd->skhd", score_grad, query_round, preferred_element_type=jnp.float32
    )
    query_grad = head_back(query_back, query_unit, query_scale, rows, features)
    key_grad = head_back(key_back, key_unit, key_scale, rows, features)
    view_term = cot_flat.astype(jnp.float32) + dot_transposed(query_grad, weights[0])
    norm_grad = dot_transposed(key_grad, weights[1]) + dot_transposed(value_gradient, weights[2])
    norm_grad = norm_grad.reshape(sides, tokens, features)
    context_term = (
        norm_grad
        - jnp.mean(norm_grad, axis=-1, keepdims=True)
        - y_hat * jnp.mean(norm_grad * y_hat, axis=-1, keepdims=True)
    ) * inv_std
    view_grads = view_term.reshape(sides, tokens, features) + context_term[::-1]
    return (decoded.reshape(sides, tokens, features), view_grads)


def per_device(encodings, image_slot, pairs, attn_weights, head_scale, cotangent):
    wide_count = lax.axis_size("wide")
    narrow_count = lax.axis_size("narrow")
    group_index = lax.axis_index("wide")
    images_here = encodings.shape[0]
    weights = lax.all_gather(attn_weights, "wide", axis=1, tiled=True)
    all_slots = jnp.take(image_slot, pairs.reshape(-1), axis=0).reshape(
        wide_count, 2 * narrow_count
    )
    all_owners = all_slots // images_here
    owned_here = all_owners == group_index
    local_index = jnp.sum(jnp.where(owned_here, all_slots % images_here, 0), axis=1)
    served = jnp.any(owned_here, axis=1)
    choose = ((local_index[:, None] == jnp.arange(images_here)[None, :]) & served[:, None]).astype(
        jnp.bfloat16
    )
    group_slots = lax.dynamic_slice_in_dim(all_slots, group_index, 1, 0)[0]
    group_owners = group_slots // images_here
    outgoing = jnp.einsum(
        "hk,krd->hrd", choose, encodings, preferred_element_type=jnp.float32
    ).astype(jnp.bfloat16)
    arriving_rows = lax.all_to_all(outgoing, "wide", split_axis=0, concat_axis=0, tiled=True)
    view_blocks = jnp.take(arriving_rows, group_owners, axis=0)
    pair_views = lax.all_to_all(view_blocks, "narrow", split_axis=0, concat_axis=1, tiled=True)
    decoded, view_grads = pair_pass(pair_views, cotangent[0], weights, head_scale)
    grad_round = view_grads.astype(jnp.bfloat16)
    back_blocks = lax.all_to_all(grad_round, "narrow", split_axis=1, concat_axis=0, tiled=True)
    route_map = (jnp.arange(wide_count)[:, None] == group_owners[None, :]).astype(jnp.bfloat16)
    outgoing_grads = jnp.einsum(
        "ov,vrd->ord", route_map, back_blocks, preferred_element_type=jnp.float32
    ).astype(jnp.bfloat16)
    returned = lax.all_to_all(outgoing_grads, "wide", split_axis=0, concat_axis=0, tiled=True)
    encoding_gradient = jnp.einsum(
        "hk,hrd->krd", choose, returned, preferred_element_type=jnp.float32
    ).astype(jnp.bfloat16)
    return (decoded[None], encoding_gradient)


def solution(mesh):
    return jax.shard_map(
        per_device,
        mesh=mesh,
        in_specs=(
            P("wide", "narrow", None),
            P(),
            P(),
            P(None, "wide", None),
            P(),
            P(("wide", "narrow"), None, None, None),
        ),
        out_specs=(P(("wide", "narrow"), None, None, None), P("wide", "narrow", None)),
        check_vma=False,
    )
```

profile of v0, /device:TPU:1, one launch (start us, length us, event | category | flops | bytes accessed | tf_op | source)
XLA Modules:
  0.0 253.1 jit_solution(14091434201810671646)
XLA Ops:
  9.1 6.6 %gather_fusion = s32[1024]{0:T(1024)S(1)} fusion(s32[128]{0:T(128)S(1)} %copy-done.1, s32[1024]{0:T(1024)S(1)} %broadcast_clamp_fusion), kind=kCustom, calls=%fused_computation | custom fusion | bytes 12288 | tf_op jit(solution)/shard_map/jit(_take)/gather | solution.py:104
  16.7 2.0 copy.79
  18.7 14.8 %all-to-all-start = ((bf16[64,16,768]{2,1,0:T(8,128)(2,1)}), bf16[64,16,768]{2,1,0:T(8,128)(2,1)S(1)}, u32[]{:S(2)}, u32[]{:S(2)}) async-start(bf16[64,16,768]{2,1,0:T(8,128)(2,1)} %copy.79), calls=%async_computation | async-start | bytes 3145728 | tf_op jit(solution)/shard_map/all_to_all | solution.py:119
  33.6 41.7 %all-to-all-done = bf16[64,16,768]{2,1,0:T(8,128)(2,1)S(1)} async-done(((bf16[64,16,768]{2,1,0:T(8,128)(2,1)}), bf16[64,16,768]{2,1,0:T(8,128)(2,1)S(1)}, u32[]{:S(2)}, u32[]{:S(2)}) %all-to-all-start) | async-done | bytes 1572896 | tf_op jit(solution)/shard_map/all_to_all | solution.py:119
  76.8 6.6 %all-to-all-start.1 = ((bf16[16,16,768]{2,1,0:T(8,128)(2,1)}), bf16[16,16,768]{2,1,0:T(8,128)(2,1)S(1)}, u32[]{:S(2)}, u32[]{:S(2)}) async-start(bf16[16,16,768]{2,1,0:T(8,128)(2,1)} %broadcast_select_fusion), calls=%async_computation.1 | async-start | bytes 786432 | tf_op jit(solution)/shard_map/all_to_all | solution.py:121
  83.4 12.4 %all-to-all-done.1 = bf16[16,16,768]{2,1,0:T(8,128)(2,1)S(1)} async-done(((bf16[16,16,768]{2,1,0:T(8,128)(2,1)}), bf16[16,16,768]{2,1,0:T(8,128)(2,1)S(1)}, u32[]{:S(2)}, u32[]{:S(2)}) %all-to-all-start.1) | async-done | bytes 393248 | tf_op jit(solution)/shard_map/all_to_all | solution.py:121
  96.4 10.0 %all-gather.2.cloned.1.call-done = bf16[4,768,768]{2,0,1:T(4,128)(2,1)} async-done(((bf16[4,12,768]{2,0,1:T(4,128)(2,1)}), bf16[4,768,768]{2,0,1:T(4,128)(2,1)}) %all-gather.2.cloned.1.call-update) | async-done | bytes 4718608 | tf_op jit(solution)/shard_map/all_gather | solution.py:103
  106.4 15.8 %fusion.76 = (bf16[1,768,768]{2,0,1:T(2,128)(2,1)}, bf16[1,768,768]{2,0,1:T(2,128)(2,1)S(1)}, bf16[1,768,768]{2,0,1:T(2,128)(2,1)}, bf16[1,768,768]{2,0,1:T(2,128)(2,1)}) fusion(bf16[4,768,768]{2,0,1:T(4,128)(2,1)} %all-gather.2.cloned.1.call-done), kind=kLoop, calls=%fused_computation.132 | loop fusion | bytes 9437184 | tf_op jit(solution)/shard_map/slice | solution.py:37
  122.3 6.4 %copy.118 = bf16[1,768,768]{1,2,0:T(8,128)(2,1)} copy(bf16[1,768,768]{2,0,1:T(2,128)(2,1)} %get-tuple-element.15) | data formatting | bytes 2359296 | tf_op jit(solution)/shard_map/dot_general | solution.py:35
  128.7 4.5 %copy.119 = bf16[1,768,768]{1,2,0:T(8,128)(2,1)} copy(bf16[1,768,768]{2,0,1:T(2,128)(2,1)S(1)} %get-tuple-element.14) | data formatting | bytes 2359296 | tf_op jit(solution)/shard_map/dot_general | solution.py:36
  133.2 2.8 %multiply_reduce_fusion.3 = (f32[2,128,12]{1,2,0:T(8,128)S(1)}, f32[2,128,12,64]{1,3,2,0:T(8,128)}) fusion(bf16[12,64,768,1]{2,1,0,3:T(8,128)(2,1)} %bitcast.148, bf16[2,128,768]{2,1,0:T(8,128)(2,1)S(1)} %fusion.29), kind=kOutput, calls=%fused_computation.51 | convolution fusion | flops 302380032 | bytes 2371584 | tf_op jit(solution)/shard_map/dot_general | solution.py:36
  136.0 1.2 convolution_convert_fusion.5
  137.2 1.9 copy.82
  139.1 1.1 reshape.228
  140.2 3.1 %convolution_convert_fusion.3 = bf16[256,768]{1,0:T(8,128)(2,1)} fusion(bf16[256,768]{1,0:T(8,128)(2,1)} %bitcast.160, bf16[1,768,768]{2,0,1:T(2,128)(2,1)} %get-tuple-element.16), kind=kOutput, calls=%fused_computation.20 | convolution fusion | flops 302186496 | bytes 1966080 | tf_op jit(solution)/shard_map/dot_general | solution.py:8
  143.3 1.9 copy.91
  145.2 1.8 reshape.230
  147.0 2.7 %multiply_reduce_fusion.4 = (f32[2,128,12]{1,2,0:T(8,128)S(1)}, f32[2,128,12,64]{1,3,2,0:T(8,128)}) fusion(bf16[2,128,768,1]{2,1,3,0:T(8,128)(2,1)S(1)} %bitcast.143, bf16[12,64,768,1]{2,1,0,3:T(8,128)(2,1)} %bitcast.147), kind=kOutput, calls=%fused_computation.52 | convolution fusion | flops 302380032 | bytes 2371584 | tf_op jit(solution)/shard_map/dot_general | solution.py:35
  149.8 1.6 fusion.52
  151.3 3.1 %fusion.35 = f32[2,12,128,128]{2,3,1,0:T(8,128)} fusion(f32[12]{0:T(128)S(1)} %broadcast_multiply_fusion.4, f32[2,128,12,64]{1,3,2,0:T(8,128)} %get-tuple-element.18, f32[2,128,12]{1,2,0:T(8,128)S(1)} %get-tuple-element.28, f32[2,128,12,64]{1,3,2,0:T(8,128)} %get-tuple-element.20, f32[2,128,12]{1,2,0:T(8,128)S(1)} %get-tuple-element.27), kind=kOutput, calls=%fused_computation.48 | convolution fusion | flops 51907712 | bytes 3170352 | tf_op jit(solution)/shard_map/div | solution.py:49
  154.5 4.8 %multiply_reduce_fusion.2 = (f32[2,128,12]{1,2,0:T(8,128)S(1)}, f32[2,128,12,64]{1,3,2,0:T(8,128)}) fusion(f32[2,128,12,64]{1,3,2,0:T(8,128)} %get-tuple-element.18, f32[2,128,12]{1,2,0:T(8,128)S(1)} %get-tuple-element.28, f32[2,12,128,128]{2,3,1,0:T(8,128)} %fusion.35, f32[2,12,128,128]{2,3,1,0:T(8,128)} %fusion.52, f32[12]{0:T(128)S(1)} %broadcast_multiply_fusion.4, ...), kind=kOutput, calls=%fused_computation.46 | convolution fusion | flops 53280896 | bytes 5541936 | tf_op jit(solution)/shard_map/shqk,skhd->sqhd/dot_general | solution.py:78
  159.3 4.9 %multiply_reduce_fusion.1 = (f32[2,128,12]{1,2,0:T(8,128)S(1)}, f32[2,128,12,64]{1,3,2,0:T(8,128)}) fusion(f32[2,128,12,64]{1,3,2,0:T(8,128)} %get-tuple-element.20, f32[2,128,12]{1,2,0:T(8,128)S(1)} %get-tuple-element.27, f32[2,12,128,128]{2,3,1,0:T(8,128)} %fusion.35, f32[2,12,128,128]{2,3,1,0:T(8,128)} %fusion.52, f32[12]{0:T(128)S(1)} %broadcast_multiply_fusion.4, ...), kind=kOutput, calls=%fused_computation.44 | convolution fusion | flops 53280896 | bytes 5541936 | tf_op jit(solution)/shard_map/shqk,sqhd->skhd/dot_general | solution.py:81
  164.2 2.3 fusion.20
  167.2 1.0 copy-done.2
  172.4 1.2 copy.101
  173.6 6.2 %all-to-all-start.2 = ((bf16[2,128,768]{2,0,1:T(2,128)(2,1)}), bf16[2,128,768]{2,0,1:T(2,128)(2,1)S(1)}, u32[]{:S(2)}, u32[]{:S(2)}) async-start(bf16[2,128,768]{2,0,1:T(2,128)(2,1)} %copy.101), calls=%async_computation.2 | async-start | bytes 786432 | tf_op jit(solution)/shard_map/all_to_all | solution.py:124
  179.8 15.1 %all-to-all-done.2 = bf16[2,128,768]{2,0,1:T(2,128)(2,1)S(1)} async-done(((bf16[2,128,768]{2,0,1:T(2,128)(2,1)}), bf16[2,128,768]{2,0,1:T(2,128)(2,1)S(1)}, u32[]{:S(2)}, u32[]{:S(2)}) %all-to-all-start.2) | async-done | bytes 393248 | tf_op jit(solution)/shard_map/all_to_all | solution.py:124
  195.7 2.0 copy.105
  197.7 6.9 %all-to-all-start.3 = ((bf16[64,16,768]{2,1,0:T(8,128)(2,1)}), bf16[64,16,768]{2,1,0:T(8,128)(2,1)}, u32[]{:S(2)}, u32[]{:S(2)}) async-start(bf16[64,16,768]{2,1,0:T(8,128)(2,1)} %copy.105), calls=%async_computation.3 | async-start | bytes 3145728 | tf_op jit(solution)/shard_map/all_to_all | solution.py:129
  206.3 1.3 fusion.18
  207.6 36.0 %all-to-all-done.3 = bf16[64,16,768]{2,1,0:T(8,128)(2,1)} async-done(((bf16[64,16,768]{2,1,0:T(8,128)(2,1)}), bf16[64,16,768]{2,1,0:T(8,128)(2,1)}, u32[]{:S(2)}, u32[]{:S(2)}) %all-to-all-start.3) | async-done | bytes 1572896 | tf_op jit(solution)/shard_map/all_to_all | solution.py:129
  243.6 2.1 fusion.22
  (73 shorter events, 12.8 us)
Async XLA Ops:
  7.2 8.9 %copy-start = (bf16[2,16,768]{2,1,0:T(8,128)(2,1)S(1)}, bf16[2,16,768]{2,1,0:T(8,128)(2,1)}, u32[]{:S(2)}) copy-start(bf16[2,16,768]{2,1,0:T(8,128)(2,1)} %param.6) | copy-start | bytes 147460
  7.2 1.9 copy-start.1
  7.2 99.3 %all-gather.2.cloned.1.call-start = ((), (), s32[]{:S(2)}) async-start(), calls=%async_computation.4 | async-start | bytes 4792320 | tf_op jit(solution)/shard_map/all_gather | solution.py:103
  18.7 56.6 %all-to-all-start = ((bf16[64,16,768]{2,1,0:T(8,128)(2,1)}), bf16[64,16,768]{2,1,0:T(8,128)(2,1)S(1)}, u32[]{:S(2)}, u32[]{:S(2)}) async-start(bf16[64,16,768]{2,1,0:T(8,128)(2,1)} %copy.79), calls=%async_computation | async-start | bytes 3145728 | tf_op jit(solution)/shard_map/all_to_all | solution.py:119
  33.6 49.8 %copy-start.13 = (f32[12]{0:T(128)S(1)}, f32[12]{0:T(128)}, u32[]{:S(2)}) copy-start(f32[12]{0:T(128)} %param.10) | copy-start | bytes 148
  76.8 19.0 %all-to-all-start.1 = ((bf16[16,16,768]{2,1,0:T(8,128)(2,1)}), bf16[16,16,768]{2,1,0:T(8,128)(2,1)S(1)}, u32[]{:S(2)}, u32[]{:S(2)}) async-start(bf16[16,16,768]{2,1,0:T(8,128)(2,1)} %broadcast_select_fusion), calls=%async_computation.1 | async-start | bytes 786432 | tf_op jit(solution)/shard_map/all_to_all | solution.py:121
  133.2 2.8 %copy-start.6 = (bf16[1,768,768]{2,0,1:T(2,128)(2,1)S(1)}, bf16[1,768,768]{2,0,1:T(2,128)(2,1)}, u32[]{:S(2)}) copy-start(bf16[1,768,768]{2,0,1:T(2,128)(2,1)} %get-tuple-element.13) | copy-start | bytes 3538948
  147.0 2.7 %copy-start.8 = (bf16[2,128,12,64]{1,0,3,2:T(2,128)(2,1)S(1)}, bf16[2,128,12,64]{1,0,3,2:T(2,128)(2,1)}, u32[]{:S(2)}) copy-start(bf16[2,128,12,64]{1,0,3,2:T(2,128)(2,1)} %reshape.230) | copy-start | bytes 1179652
  164.2 2.3 copy-start.5
  164.2 2.3 copy-start.11
  166.5 1.7 copy-start.2
  166.5 1.7 copy-start.12
  167.1 1.6 copy-start.4
  167.1 1.7 copy-start.10
  169.4 1.7 copy-start.7
  173.6 21.4 %all-to-all-start.2 = ((bf16[2,128,768]{2,0,1:T(2,128)(2,1)}), bf16[2,128,768]{2,0,1:T(2,128)(2,1)S(1)}, u32[]{:S(2)}, u32[]{:S(2)}) async-start(bf16[2,128,768]{2,0,1:T(2,128)(2,1)} %copy.101), calls=%async_computation.2 | async-start | bytes 786432 | tf_op jit(solution)/shard_map/all_to_all | solution.py:124
  197.7 6.9 %copy-start.3 = (f32[2,12,128,128]{2,3,1,0:T(8,128)S(1)}, f32[2,12,128,128]{2,3,1,0:T(8,128)}, u32[]{:S(2)}) copy-start(f32[2,12,128,128]{2,3,1,0:T(8,128)} %fusion.35) | copy-start | bytes 4718596
  197.7 45.9 %all-to-all-start.3 = ((bf16[64,16,768]{2,1,0:T(8,128)(2,1)}), bf16[64,16,768]{2,1,0:T(8,128)(2,1)}, u32[]{:S(2)}, u32[]{:S(2)}) async-start(bf16[64,16,768]{2,1,0:T(8,128)(2,1)} %copy.105), calls=%async_computation.3 | async-start | bytes 3145728 | tf_op jit(solution)/shard_map/all_to_all | solution.py:129
  204.7 1.7 copy-start.9
Sparse Core Ops, SparseCore 0:
  11.3 95.0 all-gather.1
where the time goes:
time: 254 us; the launch traced here: 253 us
  waiting for transfers between devices  116 us (46%)
  local copies, waits for them, and re-layouts  52.1 us (21%)
  starting transfers between devices  34.6 us (14%)
  matrix products  33.2 us (13%)
  between operations  14.5 us (6%)
  other arithmetic  2.84 us (1%)
    all_to_all x1, waiting for transfers between devices, per_device(): lax.all_to_all(outgoing, 'wide', split_axis=0, concat_axis=0, tiled=True)  41.7 us
    all_to_all x1, waiting for transfers between devices, per_device(): lax.all_to_all(outgoing_grads, 'wide', split_axis=0, concat_axis=0, tiled...  36 us
    slice x1, local copies, waits for them, and re-layouts, pair_pass(): value_proj = jnp.dot(y_norm, weights[2], preferred_element_type=jnp.float32)  15.8 us
    all_to_all x1, waiting for transfers between devices, per_device(): lax.all_to_all(grad_round, 'narrow', split_axis=1, concat_axis=0, tiled=T...  15.1 us
    all_to_all x1, starting transfers between devices, per_device(): lax.all_to_all(outgoing, 'wide', split_axis=0, concat_axis=0, tiled=True)  14.8 us
    all_to_all x1, waiting for transfers between devices, per_device(): lax.all_to_all(view_blocks, 'narrow', split_axis=0, concat_axis=1, tiled=...  12.4 us
    all_gather x1, waiting for transfers between devices, per_device(): weights = lax.all_gather(attn_weights, 'wide', axis=1, tiled=True)  10 us
    all_to_all x1, starting transfers between devices, per_device(): lax.all_to_all(outgoing_grads, 'wide', split_axis=0, concat_axis=0, tiled...  6.91 us
  transfers between devices with their start and end apart: 5, of which 5 were waited for; matrix products, arithmetic and copies ran while one was open for 6% of the time, Pallas kernels for 0%

commit v1 on v0

v1 whole, which is shorter than its diff:
```python
import functools

import jax
import jax.numpy as jnp
import numpy as np
from jax import lax
from jax.experimental import pallas as pl
from jax.experimental.pallas import tpu as pltpu
from jax.sharding import PartitionSpec as P

MESH = pl.DeviceIdType.MESH
BF16 = jnp.bfloat16
F32 = jnp.float32
X_SIZE = 4
CORES = 2


def dot(left, right):
    return lax.dot_general(left, right, (((1,), (0,)), ((), ())), preferred_element_type=F32)


def dot_t(left, right):
    return lax.dot_general(left, right, (((1,), (1,)), ((), ())), preferred_element_type=F32)


def t_dot(left, right):
    return lax.dot_general(left, right, (((0,), (0,)), ((), ())), preferred_element_type=F32)


class Place:
    def __init__(self, wide, narrow):
        self.xs, self.cs = X_SIZE, CORES
        self.zs, self.ys = wide // (X_SIZE * CORES), narrow
        self.w = lax.axis_index("wide")
        self.n = lax.axis_index("narrow")
        self.c = lax.rem(self.w, self.cs)
        self.x = lax.rem(self.w // self.cs, self.xs)
        self.z = self.w // (self.cs * self.xs)

    def at(self, z=None, x=None, c=None, n=None):
        z = self.z if z is None else z
        x = self.x if x is None else x
        c = self.c if c is None else c
        n = self.n if n is None else n
        return ((z * self.xs + x) * self.cs + c, n)

    def barrier(self):
        sem = pltpu.get_barrier_semaphore()
        partners = [self.at(c=1 - self.c)]
        for step in (1, -1):
            partners.append(self.at(z=lax.rem(self.z + step + self.zs, self.zs)))
            partners.append(self.at(x=lax.rem(self.x + step + self.xs, self.xs)))
        for step in range(1, self.ys):
            partners.append(self.at(n=lax.rem(self.n + step, self.ys)))
        for partner in partners:
            pl.semaphore_signal(sem, inc=1, device_id=partner, device_id_type=MESH)
        pl.semaphore_wait(sem, len(partners))


class Copies:
    def __init__(self, send, recv):
        self.send, self.recv, self.made = send, recv, []

    def start(self, src, dst, device):
        k = len(self.made)
        copy = pltpu.make_async_remote_copy(
            src_ref=src,
            dst_ref=dst,
            send_sem=self.send.at[k],
            recv_sem=self.recv.at[k],
            device_id=device,
            device_id_type=MESH,
        )
        copy.start()
        self.made.append(copy)
        return copy

    def finish(self):
        for copy in self.made:
            copy.wait_send()


def ring_gather(copies, size, pos, device, block, half, own=None, landed=None):
    plus, minus = device(lax.rem(pos + 1, size)), device(lax.rem(pos + size - 1, size))
    first = block(pos) if own is None else own
    up = copies.start(first, block(pos), plus)
    down = copies.start(first, block(pos), minus)
    if landed is not None:
        landed(pos)
    for t in range(1, size // 2):
        yield
        left, right = lax.rem(pos + size - t, size), lax.rem(pos + t, size)
        up.wait_recv()
        if t < size // 2 - 1:
            up = copies.start(block(left), block(left), plus)
        else:
            up = copies.start(half(left, 0), half(left, 0), plus)
        down.wait_recv()
        if t < size // 2 - 1:
            down = copies.start(block(right), block(right), minus)
        else:
            down = copies.start(half(right, 1), half(right, 1), minus)
        if landed is not None:
            landed(left)
            landed(right)
    yield
    up.wait_recv()
    down.wait_recv()
    if landed is not None:
        landed(lax.rem(pos + size // 2, size))


def chain(*parts):
    for part in parts:
        yield from part()


def advance(streams):
    live = []
    for stream in streams:
        try:
            next(stream)
            live.append(stream)
        except StopIteration:
            pass
    return live


def gather_kernel(
    wide, narrow, enc_ref, wpk_ref, slot_ref, x_ref, wa_ref, wb_ref,
    gx, sib_out, sib_in, stage, send, recv, local,
):
    here = Place(wide, narrow)
    zs, xs = here.zs, here.xs
    z, x, c, n = here.z, here.x, here.c, here.n
    rows = enc_ref.shape[1]
    cols = enc_ref.shape[2]
    half_cols = cols // 2
    views = 2 * narrow
    chips = zs * xs
    copies = Copies(send, recv)

    here.barrier()

    def at_z(p):
        return here.at(z=p)

    def at_x(p):
        return here.at(x=p)

    def cut(ref, h, width):
        return ref.at[:, pl.ds(h * width, width)]

    gx[z * xs + x] = enc_ref[0]
    gx[chips + x * zs + z] = enc_ref[1]
    own_a = pltpu.make_async_copy(cut(wpk_ref, 0, half_cols), wa_ref.at[c, z, x], local.at[0])
    own_b = pltpu.make_async_copy(cut(wpk_ref, 1, half_cols), wb_ref.at[c, x, z], local.at[1])
    own_a.start()
    own_b.start()

    def xa_one(p):
        return gx.at[z * xs + p]

    def xb_one(p):
        return gx.at[chips + x * zs + p]

    def xa_many(p):
        return gx.at[pl.ds(p * xs, xs)]

    def xb_many(p):
        return gx.at[pl.ds(chips + p * zs, zs)]

    def xa_part(p, h):
        return gx.at[pl.ds(p * xs + h * (xs // 2), xs // 2)]

    def xb_part(p, h):
        return gx.at[pl.ds(chips + p * zs + h * (zs // 2), zs // 2)]

    stream_xa = chain(
        lambda: ring_gather(copies, xs, x, at_x, xa_one, lambda p, h: cut(xa_one(p), h, half_cols)),
        lambda: ring_gather(copies, zs, z, at_z, xa_many, xa_part),
    )
    stream_xb = chain(
        lambda: ring_gather(copies, zs, z, at_z, xb_one, lambda p, h: cut(xb_one(p), h, half_cols)),
        lambda: ring_gather(copies, xs, x, at_x, xb_many, xb_part),
    )
    third = wpk_ref.shape[0] // 3

    def cut_rows(ref, h):
        return ref.at[pl.ds(h * third, (1 + h) * third)]

    def wa_one(p):
        return wa_ref.at[c, z, p]

    def wb_one(p):
        return wb_ref.at[c, x, p]

    def wa_many(p):
        return wa_ref.at[c, p]

    def wb_many(p):
        return wb_ref.at[c, p]

    sibling = here.at(c=1 - c)
    passed = []

    def pass_a(p):
        passed.append(copies.start(wa_many(p), wa_many(p), sibling))

    def pass_b(p):
        passed.append(copies.start(wb_many(p), wb_many(p), sibling))

    stream_wa = ring_gather(
        copies, xs, x, at_x, wa_one, lambda p, h: cut_rows(wa_one(p), h),
        own=cut(wpk_ref, 0, half_cols),
    )
    stream_wb = ring_gather(
        copies, zs, z, at_z, wb_one, lambda p, h: cut_rows(wb_one(p), h),
        own=cut(wpk_ref, 1, half_cols),
    )
    encodings = [stream_xa, stream_xb]
    weights = [stream_wa, stream_wb]
    while encodings:
        encodings = advance(encodings)
        weights = advance(weights)
    while weights:
        weights = advance(weights)
    own_a.wait()
    own_b.wait()
    weights = [
        ring_gather(
            copies, zs, z, at_z, wa_many,
            lambda p, h: wa_ref.at[c, p, pl.ds(h * (xs // 2), xs // 2)], landed=pass_a,
        ),
        ring_gather(
            copies, xs, x, at_x, wb_many,
            lambda p, h: wb_ref.at[c, p, pl.ds(h * (zs // 2), zs // 2)], landed=pass_b,
        ),
    ]
    weights = advance(weights)

    def place_of(slot):
        owner = slot // 2
        oz, ox = owner // (xs * CORES), lax.rem(owner // CORES, xs)
        first = lax.rem(slot, 2) == 0
        return lax.rem(owner, CORES), jnp.where(first, oz * xs + ox, chips + ox * zs + oz)

    for v in range(views):
        core, index = place_of(slot_ref[(1 - c) * views + v])
        sib_out[v] = gx[index]
    trade = copies.start(sib_out, sib_in, sibling)
    trade.wait_recv()
    for v in range(views):
        core, index = place_of(slot_ref[c * views + v])
        stage[v] = jnp.where(core == c, gx[index], sib_in[v])
    mine = pl.ds(pl.multiple_of(n * rows, rows), rows)
    keep = pltpu.make_async_copy(stage.at[pl.ds(2 * n, 2)], x_ref.at[:, mine, :], local.at[0])
    keep.start()
    out = []
    for step in range(1, narrow):
        m = lax.rem(n + step, narrow)
        out.append(copies.start(stage.at[pl.ds(2 * m, 2)], x_ref.at[:, mine, :], here.at(n=m)))
    while weights:
        weights = advance(weights)
    for copy in out:
        copy.wait_recv()
    for copy in passed:
        copy.wait_recv()
    keep.wait()
    copies.finish()


def gather_call(wide, narrow, enc, wpk, slots):
    zs, xs = wide // (X_SIZE * CORES), X_SIZE
    _, rows, cols = enc.shape
    views = 2 * narrow
    wrows = wpk.shape[0]
    n_copies = 4 * (zs + xs) + 1 + (narrow - 1) + zs + xs
    return pl.pallas_call(
        functools.partial(gather_kernel, wide, narrow),
        out_shape=(
            jax.ShapeDtypeStruct((2, narrow * rows, cols), BF16),
            jax.ShapeDtypeStruct((CORES, zs, xs, wrows, cols // 2), BF16),
            jax.ShapeDtypeStruct((CORES, xs, zs, wrows, cols // 2), BF16),
        ),
        in_specs=[
            pl.BlockSpec(memory_space=pltpu.VMEM),
            pl.BlockSpec(memory_space=pltpu.VMEM),
            pl.BlockSpec(memory_space=pltpu.SMEM),
        ],
        out_specs=tuple([pl.BlockSpec(memory_space=pl.ANY)] * 3),
        scratch_shapes=[
            pltpu.VMEM((2 * zs * xs, rows, cols), BF16),
            pltpu.VMEM((views, rows, cols), BF16),
            pltpu.VMEM((views, rows, cols), BF16),
            pltpu.VMEM((views, rows, cols), BF16),
            pltpu.SemaphoreType.DMA((n_copies,)),
            pltpu.SemaphoreType.DMA((n_copies,)),
            pltpu.SemaphoreType.DMA((2,)),
        ],
        compiler_params=pltpu.CompilerParams(
            collective_id=0, has_side_effects=True, vmem_limit_bytes=32 * 2**20
        ),
        name="gather_in",
    )(enc, wpk, slots)


def ring_reduce(copies, size, pos, device, parts, term, bufs, result):
    down_out, down_in, up_out, up_in = bufs
    plus, minus = device(lax.rem(pos + 1, size)), device(lax.rem(pos + size - 1, size))
    mid = size // 2
    h = parts // 2
    far = lax.rem(pos + mid, size)
    for i in range(h):
        down_out[0, i] = term(far, i).astype(BF16)
    down = copies.start(down_out.at[0, pl.ds(0, h)], down_in.at[0, pl.ds(0, h)], minus)
    for i in range(h):
        up_out[0, i] = term(far, h + i).astype(BF16)
    up = copies.start(up_out.at[0, pl.ds(0, h)], up_in.at[0, pl.ds(0, h)], plus)
    for t in range(1, mid):
        yield
        dest = lax.rem(pos + size - (mid - t), size)
        down.wait_recv()
        for i in range(parts):
            total = term(dest, i)
            if t > 1 or i < h:
                total = total + down_in[t - 1, i].astype(F32)
            down_out[t, i] = total.astype(BF16)
        down = copies.start(down_out.at[t], down_in.at[t], minus)
        dest = lax.rem(pos + (mid - t), size)
        up.wait_recv()
        for i in range(parts):
            total = term(dest, i)
            if t > 1:
                total = total + up_in[t - 1, i].astype(F32)
            elif i >= h:
                total = total + up_in[0, i - h].astype(F32)
            up_out[t, i] = total.astype(BF16)
        up = copies.start(up_out.at[t], up_in.at[t], plus)
    yield
    down.wait_recv()
    up.wait_recv()
    for i in range(parts):
        arrived = down_in[mid - 1, i].astype(F32) + up_in[mid - 1, i].astype(F32)
        result(i, term(pos, i) + arrived)


def scatter_kernel(
    wide, narrow, vg_ref, inv_ref, out_ref,
    rv, sv, res_a, res_b,
    a1, a2, a3, a4, b1, b2, b3, b4, c1, c2, c3, c4, d1, d2, d3, d4,
    send, recv, local,
):
    here = Place(wide, narrow)
    zs, xs = here.zs, here.xs
    z, x, c, n = here.z, here.x, here.c, here.n
    _, rows, cols = out_ref.shape
    half_cols = cols // 2
    views = 2 * narrow
    images = 2 * wide
    copies = Copies(send, recv)

    here.barrier()

    sibling = here.at(c=1 - c)

    def pair_rows(m):
        return pl.ds(pl.multiple_of(m * rows, rows), rows)

    mine = pl.ds(2 * n, 2)
    keep = pltpu.make_async_copy(vg_ref.at[:, pair_rows(n), :], rv.at[mine], local.at[0])
    keep.start()
    arriving = []
    for step in range(1, narrow):
        m = lax.rem(n + step, narrow)
        arriving.append(copies.start(vg_ref.at[:, pair_rows(m), :], rv.at[mine], here.at(n=m)))
    rv[views] = jnp.zeros((rows, cols), BF16)
    sv[views] = jnp.zeros((rows, cols), BF16)
    keep.wait()
    traded = [copies.start(rv.at[mine], sv.at[mine], sibling)]
    for step in range(1, narrow):
        arriving[step - 1].wait_recv()
        source = pl.ds(2 * lax.rem(n + narrow - step, narrow), 2)
        traded.append(copies.start(rv.at[source], sv.at[source], sibling))
    for copy in traded:
        copy.wait_recv()

    def term(oz, ox, k):
        slot = ((oz * xs + ox) * CORES + c) * 2 + k
        own = rv[inv_ref[c * images + slot]]
        other = sv[inv_ref[(1 - c) * images + slot]]
        return own.astype(F32) + other.astype(F32)

    def at_z(p):
        return here.at(z=p)

    def at_x(p):
        return here.at(x=p)

    def keep_a(i, value):
        res_a[i] = value

    def keep_b(i, value):
        res_b[i] = value

    def out_a(i, value):
        out_ref[0, :, i * half_cols:(i + 1) * half_cols] = value.astype(BF16)

    def out_b(i, value):
        out_ref[1, :, i * half_cols:(i + 1) * half_cols] = value.astype(BF16)

    streams = [
        chain(
            lambda: ring_reduce(
                copies, zs, z, at_z, xs, lambda p, i: term(p, i, 0), (a1, a2, a3, a4), keep_a
            ),
            lambda: ring_reduce(
                copies, xs, x, at_x, 2,
                lambda p, i: res_a[p, :, i * half_cols:(i + 1) * half_cols], (c1, c2, c3, c4), out_a,
            ),
        ),
        chain(
            lambda: ring_reduce(
                copies, xs, x, at_x, zs, lambda p, i: term(i, p, 1), (b1, b2, b3, b4), keep_b
            ),
            lambda: ring_reduce(
                copies, zs, z, at_z, 2,
                lambda p, i: res_b[p, :, i * half_cols:(i + 1) * half_cols], (d1, d2, d3, d4), out_b,
            ),
        ),
    ]
    while streams:
        streams = advance(streams)
    copies.finish()


def scatter_call(wide, narrow, view_grad, inverse):
    zs, xs = wide // (X_SIZE * CORES), X_SIZE
    _, tokens, cols = view_grad.shape
    rows = tokens // narrow
    views = 2 * narrow
    n_copies = (narrow - 1) + narrow + 2 * (zs + xs)
    bufs = (
        [pltpu.VMEM((zs // 2, xs, rows, cols), BF16)] * 4
        + [pltpu.VMEM((xs // 2, zs, rows, cols), BF16)] * 4
        + [pltpu.VMEM((xs // 2, 2, rows, cols // 2), BF16)] * 4
        + [pltpu.VMEM((zs // 2, 2, rows, cols // 2), BF16)] * 4
    )
    return pl.pallas_call(
        functools.partial(scatter_kernel, wide, narrow),
        out_shape=jax.ShapeDtypeStruct((2, rows, cols), BF16),
        in_specs=[
            pl.BlockSpec(memory_space=pl.ANY),
            pl.BlockSpec(memory_space=pltpu.SMEM),
        ],
        out_specs=pl.BlockSpec(memory_space=pltpu.VMEM),
        scratch_shapes=[
            pltpu.VMEM((views + 1, rows, cols), BF16),
            pltpu.VMEM((views + 1, rows, cols), BF16),
            pltpu.VMEM((xs, rows, cols), F32),
            pltpu.VMEM((zs, rows, cols), F32),
            *bufs,
            pltpu.SemaphoreType.DMA((n_copies,)),
            pltpu.SemaphoreType.DMA((n_copies,)),
            pltpu.SemaphoreType.DMA((1,)),
        ],
        compiler_params=pltpu.CompilerParams(
            collective_id=1, has_side_effects=True, vmem_limit_bytes=32 * 2**20
        ),
        name="scatter_out",
    )(view_grad, inverse)


def order_rows(owners, per_owner, mats):
    count = owners * per_owner * mats
    table = np.zeros((count, count), np.float32)
    for i in range(mats):
        for o in range(owners):
            for r in range(per_owner):
                table[(i * owners + o) * per_owner + r, (o * mats + i) * per_owner + r] = 1.0
    return table


def head_sums(width):
    half = width // 2
    row = (np.arange(2 * width) % width) // half
    col = np.arange(width) // half
    return (row[:, None] == col[None, :]).astype(np.float32)


def compute_kernel(
    x_ref, wa_ref, wb_ref, order_ref, sums_ref, scale_ref, cot_ref, dec_ref, vg_ref,
    w, q_s, k_s, v_s, ag_s, att_s, qg_s, kg_s, vgr_s,
):
    sides, tokens, cols = x_ref.shape
    heads = scale_ref.shape[0]
    head_dim = cols // heads
    block = 2 * head_dim
    rows = sides * tokens
    _, zs, xs, wrows, half_cols = wa_ref.shape
    mats = 4
    owner_rows = wrows // mats
    owners = order_ref.shape[0] // wrows
    group_rows = owners * owner_rows

    order = order_ref[...]
    for q in range(zs * xs * CORES // owners):
        for part, ref in ((0, wa_ref), (1, wb_ref)):
            pieces = []
            for o in range(q * owners, (q + 1) * owners):
                oc, ox, oz = o % CORES, (o // CORES) % xs, o // (CORES * xs)
                pieces.append(ref[oc, oz, ox] if part == 0 else ref[oc, ox, oz])
            ordered = dot(order, jnp.concatenate(pieces, axis=0)).astype(BF16)
            for i in range(mats):
                w[i, q * group_rows:(q + 1) * group_rows, part * half_cols:(part + 1) * half_cols] = (
                    ordered[i * group_rows:(i + 1) * group_rows]
                )

    views = x_ref[...].reshape(rows, cols)
    cot = cot_ref[...].reshape(rows, cols)
    views_f = views.astype(F32)
    centred = views_f - jnp.mean(views_f, axis=-1, keepdims=True)
    inv_std = lax.rsqrt(jnp.mean(centred * centred, axis=-1, keepdims=True) + 1e-06)
    y_hat = centred * inv_std
    y_norm = y_hat.astype(BF16)
    q_s[...] = dot(views, w[0])
    k_s[...] = dot(y_norm, w[1])
    v_s[...] = dot(y_norm, w[2]).astype(BF16)
    ag_s[...] = dot_t(cot, w[3]).astype(BF16)

    sums = sums_ref[...]

    def head_mean(value):
        high = value.astype(BF16)
        low = (value - high.astype(F32)).astype(BF16)
        return dot(jnp.concatenate([high, low], axis=1), sums) * (1.0 / head_dim)

    lane = lax.broadcasted_iota(jnp.int32, (tokens, block), 1)
    first = lane < head_dim

    def stack(value):
        zero = jnp.zeros_like(value)
        return jnp.concatenate([jnp.where(first, value, zero), jnp.where(first, zero, value)], axis=0)

    def unstack(value):
        return jnp.where(first, value[:tokens], value[tokens:])

    for hp in range(heads // 2):
        cb = slice(hp * block, (hp + 1) * block)
        query = q_s[:, cb]
        key = k_s[:, cb]
        q_inv = lax.rsqrt(head_mean(query * query) + 1e-06)
        k_inv = lax.rsqrt(head_mean(key * key) + 1e-06)
        q_unit = query * q_inv
        k_unit = key * k_inv
        q_round = q_unit.astype(BF16)
        k_round = k_unit.astype(BF16)
        value = v_s[:, cb]
        a_grad = ag_s[:, cb]
        row = lax.broadcasted_iota(jnp.int32, (2 * tokens, 1), 0)
        factor = jnp.where(row < tokens, scale_ref[2 * hp], scale_ref[2 * hp + 1]) / head_dim
        q_backs, k_backs = [None] * sides, [None] * sides
        for s in range(sides):
            mine = slice(s * tokens, (s + 1) * tokens)
            other = slice((1 - s) * tokens, (2 - s) * tokens)
            q2, a2 = stack(q_round[mine]), stack(a_grad[mine])
            kt, vt = k_round[other], value[other]
            e = jnp.exp(dot_t(q2, kt) * factor)
            probs = e / jnp.sum(e, axis=-1, keepdims=True)
            p_round = probs.astype(BF16)
            att_s[mine, cb] = unstack(dot(p_round, vt)).astype(BF16)
            p_grad = dot_t(a2, vt)
            s_grad = probs * (p_grad - jnp.sum(probs * p_grad, axis=-1, keepdims=True)) * factor
            s_grad = s_grad.astype(BF16)
            vgr_s[other, cb] = t_dot(p_round, a2).astype(BF16)
            q_backs[s] = unstack(dot(s_grad, kt))
            k_backs[1 - s] = t_dot(s_grad, q2)
        q_back = jnp.concatenate(q_backs, axis=0)
        k_back = jnp.concatenate(k_backs, axis=0)
        qg_s[:, cb] = ((q_back - q_unit * head_mean(q_back * q_unit)) * q_inv).astype(BF16)
        kg_s[:, cb] = ((k_back - k_unit * head_mean(k_back * k_unit)) * k_inv).astype(BF16)

    decoded = (views_f + dot(att_s[...], w[3])).astype(BF16)
    dec_ref[...] = decoded.reshape(sides, tokens, cols)
    view_term = cot.astype(F32) + dot_t(qg_s[...], w[0])
    norm_grad = dot_t(kg_s[...], w[1]) + dot_t(vgr_s[...], w[2])
    context_term = (
        norm_grad
        - jnp.mean(norm_grad, axis=-1, keepdims=True)
        - y_hat * jnp.mean(norm_grad * y_hat, axis=-1, keepdims=True)
    ) * inv_std
    vg_ref[...] = (view_term + context_term).astype(BF16).reshape(sides, tokens, cols)


def compute_call(x, wa, wb, head_scale, cot):
    sides, tokens, cols = x.shape
    heads = head_scale.shape[0]
    rows = sides * tokens
    _, zs, xs, wrows, _ = wa.shape
    owners = 4
    order = jnp.asarray(order_rows(owners, wrows // 4, 4), BF16)
    sums = jnp.asarray(head_sums(2 * cols // heads), BF16)
    vmem = pl.BlockSpec(memory_space=pltpu.VMEM)
    shape = jax.ShapeDtypeStruct(x.shape, BF16)
    return pl.pallas_call(
        compute_kernel,
        out_shape=(shape, shape),
        in_specs=[vmem] * 5 + [pl.BlockSpec(memory_space=pltpu.SMEM), vmem],
        out_specs=(vmem, vmem),
        scratch_shapes=[
            pltpu.VMEM((4, cols, cols), BF16),
            pltpu.VMEM((rows, cols), F32),
            pltpu.VMEM((rows, cols), F32),
        ] + [pltpu.VMEM((rows, cols), BF16)] * 6,
        compiler_params=pltpu.CompilerParams(vmem_limit_bytes=56 * 2**20),
        cost_estimate=pl.CostEstimate(
            flops=16 * rows * cols * cols, bytes_accessed=10 * 2**20, transcendentals=rows * 2 * cols
        ),
        name="pair_pass",
    )(x, wa, wb, order, sums, head_scale, cot)


def per_device(encodings, image_slot, pairs, attn_weights, head_scale, cotangent):
    wide = lax.axis_size("wide")
    narrow = lax.axis_size("narrow")
    chip = lax.axis_index("wide") // CORES
    images = image_slot.shape[0]
    views = 2 * narrow
    chip_pairs = lax.dynamic_slice_in_dim(pairs, chip * CORES * narrow, CORES * narrow, 0)
    chip_pairs = chip_pairs.reshape(CORES * views)
    every = jnp.arange(images, dtype=jnp.int32)
    slots = jnp.sum(jnp.where(chip_pairs[:, None] == every[None, :], image_slot[None, :], 0), axis=1)
    by_core = slots.reshape(CORES, views, 1)
    view = jnp.arange(views, dtype=jnp.int32)[None, :, None]
    inverse = views + jnp.sum(jnp.where(by_core == every[None, None, :], view - views, 0), axis=1)
    mats, wrows, cols = attn_weights.shape
    wpk = attn_weights.reshape(mats * wrows, cols)
    x, wa, wb = gather_call(wide, narrow, encodings, wpk, slots)
    decoded, view_grad = compute_call(x, wa, wb, head_scale, cotangent[0])
    encoding_gradient = scatter_call(wide, narrow, view_grad, inverse.reshape(CORES * images))
    return (decoded[None], encoding_gradient)


def solution(mesh):
    return jax.shard_map(
        per_device,
        mesh=mesh,
        in_specs=(
            P("wide", "narrow", None),
            P(),
            P(),
            P(None, "wide", None),
            P(),
            P(("wide", "narrow"), None, None, None),
        ),
        out_specs=(P(("wide", "narrow"), None, None, None), P("wide", "narrow", None)),
        check_vma=False,
    )
```

time: 254 us -> 128 us (0.50)
  Pallas kernels: 0 us -> 117 us
  waiting for transfers between devices: 116 us -> 0 us
  local copies, waits for them, and re-layouts: 52.1 us -> 7.9 us
  starting transfers between devices: 34.6 us -> 0 us
  matrix products: 33.2 us -> 0 us
  between operations: 14.5 us -> 0.71 us
    pallas_call x0 -> x3, Pallas kernels: none -> 117 us  [the longest x1 62.5 us: gather_call(): pl.pallas_call(functools.partial(gather_kernel, wide, narrow), out_shape=...]
    all_to_all x4 -> x0, waiting for transfers between devices: 105 us -> none  [the longest x1 41.7 us: per_device(): lax.all_to_all(outgoing, 'wide', split_axis=0, concat_axis=0, tiled=True)]
    all_to_all x4 -> x0, starting transfers between devices: 34.5 us -> none  [the longest x1 14.8 us: per_device(): lax.all_to_all(outgoing, 'wide', split_axis=0, concat_axis=0, tiled=True)]
    dot_general x16 -> x0, matrix products: 30 us -> none  [the longest x1 4.89 us: pair_pass(): jnp.einsum('shqk,sqhd->skhd', score_grad, query_round, preferred_element_...]
    slice x1 -> x0, local copies, waits for them, and re-layouts: 15.8 us -> none  [pair_pass(): value_proj = jnp.dot(y_norm, weights[2], preferred_element_type=jnp.float32)]
    dot_general x2 -> x0, local copies, waits for them, and re-layouts: 10.9 us -> none  [the longest x1 6.42 us: pair_pass(): jnp.dot(flat_views, weights[0], preferred_element_type=jnp.float32)]
    convert_element_type x9 -> x0, local copies, waits for them, and re-layouts: 10.6 us -> none  [the longest x1 2.04 us: per_device(): outgoing = jnp.einsum('hk,krd->hrd', choose, encodings, preferred_element...]
    all_gather x1 -> x0, waiting for transfers between devices: 10 us -> none  [per_device(): weights = lax.all_gather(attn_weights, 'wide', axis=1, tiled=True)]
  transfers between devices with their start and end apart: 5 -> 0, of which waited for: 5 -> 0; matrix products, arithmetic and copies ran while one was open for 6% -> 0% of each run, Pallas kernels for 0% -> 0%
where the time goes in v1:
time: 128 us; the launch traced here: 126 us
  Pallas kernels  117 us (91%)
  local copies, waits for them, and re-layouts  7.9 us (6%)
    pallas_call x1, Pallas kernels, gather_call(): pl.pallas_call(functools.partial(gather_kernel, wide, narrow), out_shape=...  62.5 us
    pallas_call x1, Pallas kernels, scatter_call(): pl.pallas_call(functools.partial(scatter_kernel, wide, narrow), out_shape...  39.4 us
    pallas_call x1, Pallas kernels, compute_call(): pl.pallas_call(compute_kernel, out_shape=(shape, shape), in_specs=[vmem]...  14.7 us
    unnamed x14, local copies, waits for them, and re-layouts  7.56 us

profile of v1, /device:TPU:1, one launch (start us, length us, event | category | flops | bytes accessed | tf_op | source)
XLA Modules:
  0.0 126.2 jit_solution(8029724475732659990)
XLA Ops:
  0.6 0.0 copy-start
  0.7 0.7 copy-done
  1.3 0.1 constant_dynamic-slice_fusion
  1.4 0.1 copy.15
  1.5 0.1 eq.30
  1.6 0.8 select_reduce_fusion.1.slot_ref
  2.4 0.9 copy.14
  3.3 0.0 copy-start.2
  3.4 0.8 copy-done.2
  4.1 62.5 %gather_in.1 = (bf16[2,128,768]{2,1,0:T(8,128)(2,1)S(1)}, bf16[2,8,4,48,384]{4,3,2,1,0:T(8,128)(2,1)S(1)}, bf16[2,4,8,48,384]{4,3,2,1,0:T(8,128)(2,1)S(1)}) custom-call(bf16[2,16,768]{2,1,0:T(8,128)(2,1)S(1)} %copy-done.2, bf16[48,768]{1,0:T(8,128)(2,1)S(1)} %reshape.20.wpk_ref, s32[32]{0:T(128)S(1)} %select_reduce_fusion.1.slot_ref), custom_call_target="tpu_custom_call" | custom-call | tf_op jit(solution)/shard_map/gather_in/pallas_call | solution.py:279
  66.7 0.0 copy-start.3
  66.7 1.4 %copy-done.3 = bf16[2,8,4,48,384]{4,3,2,1,0:T(8,128)(2,1)} copy-done((bf16[2,8,4,48,384]{4,3,2,1,0:T(8,128)(2,1)}, bf16[2,8,4,48,384]{4,3,2,1,0:T(8,128)(2,1)S(1)}, u32[]{:S(2)}) %copy-start.3) | copy-done | bytes 2359320
  68.1 0.0 copy-start.4
  68.1 1.4 %copy-done.4 = bf16[2,4,8,48,384]{4,3,2,1,0:T(8,128)(2,1)} copy-done((bf16[2,4,8,48,384]{4,3,2,1,0:T(8,128)(2,1)}, bf16[2,4,8,48,384]{4,3,2,1,0:T(8,128)(2,1)S(1)}, u32[]{:S(2)}) %copy-start.4) | copy-done | bytes 2359320
  69.5 0.0 copy-start.5
  69.5 0.8 copy-done.5
  70.2 14.7 %pair_pass.1 = (bf16[2,128,768]{2,1,0:T(8,128)(2,1)}, bf16[2,128,768]{2,1,0:T(8,128)(2,1)}) custom-call(bf16[2,128,768]{2,1,0:T(8,128)(2,1)} %copy-done.5, bf16[2,8,4,48,384]{4,3,2,1,0:T(8,128)(2,1)} %copy-done.3, bf16[2,4,8,48,384]{4,3,2,1,0:T(8,128)(2,1)} %copy-done.4, bf16[192,192]{1,0:T(8,128)(2,1)} %constant.34.clone.order_ref, ...), custom_call_target="tpu_custom_call" | custom-call | flops 2415919104 | bytes 10485760 | tf_op jit(solution)/shard_map/pair_pass/pallas_call | solution.py:605
  84.9 0.1 eq.34
  85.0 0.1 select_reduce_fusion
  85.1 0.0 copy-start.1
  85.1 1.0 copy-done.1
  86.1 39.4 %scatter_out.1 = bf16[2,16,768]{2,1,0:T(8,128)(2,1)S(1)} custom-call(bf16[2,128,768]{2,1,0:T(8,128)(2,1)S(1)} %copy-done.1, s32[256]{0:T(256)S(1)} %add_bitcast_fusion.inv_ref), custom_call_target="tpu_custom_call" | custom-call | tf_op jit(solution)/shard_map/scatter_out/pallas_call | solution.py:449
  125.6 0.6 copy.17
  (3 shorter events, 0.0 us)
Async XLA Ops:
  0.6 0.7 copy-start
  3.3 0.8 copy-start.2
  66.7 1.4 %copy-start.3 = (bf16[2,8,4,48,384]{4,3,2,1,0:T(8,128)(2,1)}, bf16[2,8,4,48,384]{4,3,2,1,0:T(8,128)(2,1)S(1)}, u32[]{:S(2)}) copy-start(bf16[2,8,4,48,384]{4,3,2,1,0:T(8,128)(2,1)S(1)} %get-tuple-element.8.wa_ref) | copy-start | bytes 7077892
  68.1 1.4 %copy-start.4 = (bf16[2,4,8,48,384]{4,3,2,1,0:T(8,128)(2,1)}, bf16[2,4,8,48,384]{4,3,2,1,0:T(8,128)(2,1)S(1)}, u32[]{:S(2)}) copy-start(bf16[2,4,8,48,384]{4,3,2,1,0:T(8,128)(2,1)S(1)} %get-tuple-element.9.wb_ref) | copy-start | bytes 7077892
  69.5 0.8 copy-start.5
  85.1 1.0 copy-start.1

commit v2 on v0

v2 whole, which is shorter than its diff:
```python
import functools

import jax
import jax.numpy as jnp
import numpy as np
from jax import lax
from jax.experimental import pallas as pl
from jax.experimental.pallas import tpu as pltpu
from jax.sharding import PartitionSpec as P

MESH = pl.DeviceIdType.MESH
BF16 = jnp.bfloat16
F32 = jnp.float32
X_SIZE = 4
CORES = 2


def dot(left, right):
    return lax.dot_general(left, right, (((1,), (0,)), ((), ())), preferred_element_type=F32)


def dot_t(left, right):
    return lax.dot_general(left, right, (((1,), (1,)), ((), ())), preferred_element_type=F32)


def t_dot(left, right):
    return lax.dot_general(left, right, (((0,), (0,)), ((), ())), preferred_element_type=F32)


class Place:
    def __init__(self, wide, narrow):
        self.xs, self.cs = X_SIZE, CORES
        self.zs, self.ys = wide // (X_SIZE * CORES), narrow
        self.w = lax.axis_index("wide")
        self.n = lax.axis_index("narrow")
        self.c = lax.rem(self.w, self.cs)
        self.x = lax.rem(self.w // self.cs, self.xs)
        self.z = self.w // (self.cs * self.xs)

    def at(self, z=None, x=None, c=None, n=None):
        z = self.z if z is None else z
        x = self.x if x is None else x
        c = self.c if c is None else c
        n = self.n if n is None else n
        return ((z * self.xs + x) * self.cs + c, n)

    def ring(self, axis, step):
        if axis == "z":
            return self.at(z=lax.rem(self.z + step, self.zs))
        if axis == "x":
            return self.at(x=lax.rem(self.x + step, self.xs))
        return self.at(n=lax.rem(self.n + step, self.ys))

    def barrier(self):
        sem = pltpu.get_barrier_semaphore()
        partners = [self.at(c=1 - self.c)]
        for axis, size in (("z", self.zs), ("x", self.xs)):
            for step in range(1, size):
                w, n = self.ring(axis, step)
                partners.append((w, n))
                partners.append((w + 1 - 2 * self.c, n))
        for step in range(1, self.ys):
            partners.append(self.ring("y", step))
        for partner in partners:
            pl.semaphore_signal(sem, inc=1, device_id=partner, device_id_type=MESH)
        pl.semaphore_wait(sem, len(partners))


def outward(size):
    return sorted(range(1, size), key=lambda step: -min(step, size - step))


class Copies:
    def __init__(self, send, recv):
        self.send, self.recv, self.made = send, recv, []

    def start(self, src, dst, device):
        k = len(self.made)
        copy = pltpu.make_async_remote_copy(
            src_ref=src,
            dst_ref=dst,
            send_sem=self.send.at[k],
            recv_sem=self.recv.at[k],
            device_id=device,
            device_id_type=MESH,
        )
        copy.start()
        self.made.append(copy)
        return copy

    def finish(self):
        for copy in self.made:
            copy.wait_send()


def ring_gather(copies, size, pos, device, block, half, own=None, landed=None):
    plus, minus = device(lax.rem(pos + 1, size)), device(lax.rem(pos + size - 1, size))
    first = block(pos) if own is None else own
    up = copies.start(first, block(pos), plus)
    down = copies.start(first, block(pos), minus)
    if landed is not None:
        landed(pos)
    for t in range(1, size // 2):
        yield
        left, right = lax.rem(pos + size - t, size), lax.rem(pos + t, size)
        up.wait_recv()
        if t < size // 2 - 1:
            up = copies.start(block(left), block(left), plus)
        else:
            up = copies.start(half(left, 0), half(left, 0), plus)
        down.wait_recv()
        if t < size // 2 - 1:
            down = copies.start(block(right), block(right), minus)
        else:
            down = copies.start(half(right, 1), half(right, 1), minus)
        if landed is not None:
            landed(left)
            landed(right)
    yield
    up.wait_recv()
    down.wait_recv()
    if landed is not None:
        landed(lax.rem(pos + size // 2, size))


class Chunk:
    def __init__(self, here, copies, kind, lo, width, pick, view_at, bufs):
        self.here, self.copies = here, copies
        self.cols = pl.ds(lo, width)
        self.lo, self.hi = lo, lo + width
        self.axes = "xz" if kind == "x first" else "zx"
        place = {"x": (here.x, here.xs), "z": (here.z, here.zs)}
        (self.at1, self.size1), (self.at2, self.size2) = place[self.axes[0]], place[self.axes[1]]
        self.pick, self.view_at = pick, view_at
        (self.near, self.out2, self.in2, self.back, self.bout2, self.bin2, self.sums, self.last) = bufs

    @staticmethod
    def shapes(kind, zs, xs, views, rows, width):
        size1, size2 = (xs, zs) if kind == "x first" else (zs, xs)
        ends = (size1, 2, rows, width)
        routed = (size2, CORES, size1, rows, width)
        return [ends, routed, routed, (views + 1, rows, width), routed, routed, ends, ends]

    def wide(self, i1, i2, core):
        at = {self.axes[0]: i1, self.axes[1]: i2}
        return self.here.at(c=core, **at)[0]

    def target(self, i2, core):
        return self.here.at(c=core, **{self.axes[1]: i2})

    def second_places(self):
        return [(s, lax.rem(self.at2 + s, self.size2)) for s in outward(self.size2) + [0]]

    def route(self, outgoing, incoming, block):
        c, started = self.here.c, []
        for s, p in self.second_places():
            for core in range(CORES):
                for i in range(self.size1):
                    outgoing[p, core, i] = block(i, p, core)
            for core in (c, 1 - c) if s else (1 - c,):
                started.append(
                    self.copies.start(
                        outgoing.at[p, core], incoming.at[self.at2, c], self.target(p, core)
                    )
                )
            if s == 0:
                incoming[self.at2, c] = outgoing[self.at2, c]
        return started

    def gather_first(self, enc_ref):
        self.started = [
            self.copies.start(
                enc_ref.at[:, :, self.cols], self.near.at[self.at1], self.here.ring(self.axes[0], s)
            )
            for s in outward(self.size1)
        ]
        self.near[self.at1] = enc_ref[:, :, self.lo:self.hi]

    def gather_second(self):
        for copy in self.started:
            copy.wait_recv()
        c = self.here.c

        def chosen(i, p, core):
            owner = self.wide(i, self.at2, c)
            group = self.wide(self.at1, p, core)
            return self.near[i, self.pick(owner, group)]

        self.started = self.route(self.out2, self.in2, chosen)

    def gather_third(self, slot_ref, stage, views_ref, rows):
        for copy in self.started:
            copy.wait_recv()
        here, n = self.here, self.here.n
        for v in range(2 * here.ys):
            owner = slot_ref[v] // 2
            oc, ox, oz = lax.rem(owner, CORES), lax.rem(owner // CORES, here.xs), owner // (CORES * here.xs)
            o1, o2 = (ox, oz) if self.axes[0] == "x" else (oz, ox)
            stage[v, :, self.lo:self.hi] = self.in2[o2, oc, o1]
        mine = pl.ds(pl.multiple_of(n * rows, rows), rows)
        self.started = []
        for s in outward(here.ys):
            m = lax.rem(n + s, here.ys)
            self.started.append(
                self.copies.start(
                    stage.at[pl.ds(2 * m, 2), :, self.cols], views_ref.at[:, mine, self.cols], here.at(n=m)
                )
            )
        for side in range(2):
            views_ref[side, mine, self.lo:self.hi] = stage[2 * n + side, :, self.lo:self.hi]

    def wait(self):
        for copy in self.started:
            copy.wait_recv()

    def scatter_first(self, grad_ref, rows):
        here, n = self.here, self.here.n
        mine = pl.ds(2 * n, 2)
        self.started = []
        for s in outward(here.ys):
            m = lax.rem(n + s, here.ys)
            theirs = pl.ds(pl.multiple_of(m * rows, rows), rows)
            self.started.append(
                self.copies.start(grad_ref.at[:, theirs, self.cols], self.back.at[mine], here.at(n=m))
            )
        own = pl.ds(pl.multiple_of(n * rows, rows), rows)
        for side in range(2):
            self.back[2 * n + side] = grad_ref[side, own, self.lo:self.hi]

    def scatter_second(self):
        self.wait()

        def term(i, p, core):
            return self.back[self.view_at(self.wide(i, p, core))]

        self.started = self.route(self.bout2, self.bin2, term)

    def scatter_third(self):
        self.wait()
        here, c = self.here, self.here.c
        self.started = []
        for s in outward(self.size1) + [0]:
            i = lax.rem(self.at1 + s, self.size1)
            totals = [jnp.zeros(self.bin2.shape[3:], F32)] * 2
            owner = self.wide(i, self.at2, c)
            for p in range(self.size2):
                for core in range(CORES):
                    block = self.bin2[p, core, i].astype(F32)
                    image = self.pick(owner, self.wide(self.at1, p, core))
                    totals[0] = totals[0] + jnp.where(image == 0, block, 0.0)
                    totals[1] = totals[1] + jnp.where(image == 0, 0.0, block)
            if s == 0:
                self.own = totals
                continue
            for k in range(2):
                self.sums[i, k] = totals[k].astype(BF16)
            self.started.append(
                self.copies.start(
                    self.sums.at[i], self.last.at[self.at1], here.ring(self.axes[0], s)
                )
            )

    def scatter_end(self, out_ref):
        self.wait()
        for k in range(2):
            total = self.own[k]
            for s in range(1, self.size1):
                total = total + self.last[lax.rem(self.at1 + s, self.size1), k].astype(F32)
            out_ref[k, :, self.lo:self.hi] = total.astype(BF16)


class Weights:
    def __init__(self, here, copies, rows_ref, wy, wz, bcast_send, bcast_recv):
        self.here, self.copies = here, copies
        self.half = rows_ref.shape[1] // 2
        self.src_y = rows_ref.at[:, pl.ds(0, self.half)]
        self.src_z = rows_ref.at[:, pl.ds(self.half, self.half)]
        self.rows_ref, self.wy, self.wz = rows_ref, wy, wz
        self.bcast_send, self.bcast_recv = bcast_send, bcast_recv
        self.passed = []

    def from_z(self, s):
        here = self.here
        return pltpu.make_async_remote_copy(
            src_ref=self.src_y,
            dst_ref=self.wy.at[here.n, here.c, here.x],
            send_sem=self.bcast_send.at[s - 1],
            recv_sem=self.bcast_recv,
            device_id=here.ring("z", s),
            device_id_type=MESH,
        )

    def start(self):
        here, copies = self.here, self.copies

        @pl.when(here.z == here.n)
        def _():
            for s in outward(here.zs):
                self.from_z(s).start()
            self.wy[here.n, here.c, here.x] = self.rows_ref[:, :self.half]

        self.along_z = [
            copies.start(self.src_z, self.wz.at[here.c, here.x, here.z], here.ring("z", s))
            for s in outward(here.zs)
        ]
        self.wz[here.c, here.x, here.z] = self.rows_ref[:, self.half:]

    def second_y(self):
        here = self.here

        @pl.when(here.z != here.n)
        def _():
            self.from_z(1).wait_recv()

        block = self.wy.at[here.n, here.c, here.x]
        self.along_x = [self.copies.start(block, block, here.ring("x", s)) for s in outward(here.xs)]

    def rounds_y(self):
        here, copies = self.here, self.copies
        for copy in self.along_x:
            copy.wait_recv()

        def block(p):
            return self.wy.at[p, here.c]

        def half(p, h):
            return self.wy.at[p, here.c, pl.ds(h * (here.xs // 2), here.xs // 2)]

        yield from ring_gather(
            copies, here.ys, here.n, lambda p: here.at(n=p), block, half, landed=self.hand_on(block)
        )

    def rounds_z(self):
        here, copies = self.here, self.copies
        for copy in self.along_z:
            copy.wait_recv()

        def block(p):
            return self.wz.at[here.c, p]

        def half(p, h):
            return self.wz.at[here.c, p, pl.ds(h * (here.zs // 2), here.zs // 2)]

        yield from ring_gather(
            copies, here.xs, here.x, lambda p: here.at(x=p), block, half, landed=self.hand_on(block)
        )

    def hand_on(self, block):
        sibling = self.here.at(c=1 - self.here.c)

        def landed(p):
            self.passed.append(self.copies.start(block(p), block(p), sibling))

        return landed

    def finish(self):
        for copy in self.passed:
            copy.wait_recv()

        @pl.when(self.here.z == self.here.n)
        def _():
            for s in outward(self.here.zs):
                self.from_z(s).wait_send()


def order_rows(owners, per_owner, mats):
    count = owners * per_owner * mats
    table = np.zeros((count, count), np.float32)
    for i in range(mats):
        for o in range(owners):
            for r in range(per_owner):
                table[(i * owners + o) * per_owner + r, (o * mats + i) * per_owner + r] = 1.0
    return table


def head_sums(width):
    half = width // 2
    row = (np.arange(2 * width) % width) // half
    col = np.arange(width) // half
    return (row[:, None] == col[None, :]).astype(np.float32)


def order_weights(wy, wz, order_ref, w):
    zs, cores, xs, wrows, half = wy.shape
    mats = w.shape[0]
    order = order_ref[...]
    owners = order.shape[0] // wrows
    group_rows = order.shape[0] // mats
    for q in range(zs * xs * cores // owners):
        for part in range(2):
            pieces = []
            for o in range(q * owners, (q + 1) * owners):
                oc, ox, oz = o % cores, (o // cores) % xs, o // (cores * xs)
                pieces.append(wy[oz, oc, ox] if part == 0 else wz[oc, ox, oz])
            ordered = dot(order, jnp.concatenate(pieces, axis=0)).astype(BF16)
            for i in range(mats):
                w[i, q * group_rows:(q + 1) * group_rows, part * half:(part + 1) * half] = (
                    ordered[i * group_rows:(i + 1) * group_rows]
                )


def pair_pass(
    x_ref, w, sums_ref, scale_ref, cot_ref, dec_ref, vg_ref, q_s, k_s, v_s, ag_s, att_s, qg_s, kg_s, vgr_s
):
    sides, tokens, cols = x_ref.shape
    heads = scale_ref.shape[0]
    head_dim = cols // heads
    block = 2 * head_dim
    rows = sides * tokens
    views = x_ref[...].reshape(rows, cols)
    cot = cot_ref[...].reshape(rows, cols)
    views_f = views.astype(F32)
    centred = views_f - jnp.mean(views_f, axis=-1, keepdims=True)
    inv_std = lax.rsqrt(jnp.mean(centred * centred, axis=-1, keepdims=True) + 1e-06)
    y_hat = centred * inv_std
    y_norm = y_hat.astype(BF16)
    q_s[...] = dot(views, w[0])
    k_s[...] = dot(y_norm, w[1])
    v_s[...] = dot(y_norm, w[2]).astype(BF16)

    sums = sums_ref[...]

    def head_mean(value):
        high = value.astype(BF16)
        low = (value - high.astype(F32)).astype(BF16)
        return dot(jnp.concatenate([high, low], axis=1), sums) * (1.0 / head_dim)

    lane = lax.broadcasted_iota(jnp.int32, (tokens, block), 1)
    first = lane < head_dim

    def stack(value):
        zero = jnp.zeros_like(value)
        return jnp.concatenate([jnp.where(first, value, zero), jnp.where(first, zero, value)], axis=0)

    def unstack(value):
        return jnp.where(first, value[:tokens], value[tokens:])

    for hp in range(heads // 2):
        cb = slice(hp * block, (hp + 1) * block)
        query = q_s[:, cb]
        key = k_s[:, cb]
        q_inv = lax.rsqrt(head_mean(query * query) + 1e-06)
        k_inv = lax.rsqrt(head_mean(key * key) + 1e-06)
        q_unit = query * q_inv
        k_unit = key * k_inv
        q_round = q_unit.astype(BF16)
        k_round = k_unit.astype(BF16)
        value = v_s[:, cb]
        a_grad = ag_s[:, cb]
        row = lax.broadcasted_iota(jnp.int32, (2 * tokens, 1), 0)
        factor = jnp.where(row < tokens, scale_ref[2 * hp], scale_ref[2 * hp + 1]) / head_dim
        q_backs, k_backs = [None] * sides, [None] * sides
        for s in range(sides):
            mine = slice(s * tokens, (s + 1) * tokens)
            other = slice((1 - s) * tokens, (2 - s) * tokens)
            q2, a2 = stack(q_round[mine]), stack(a_grad[mine])
            kt, vt = k_round[other], value[other]
            e = jnp.exp(dot_t(q2, kt) * factor)
            probs = e / jnp.sum(e, axis=-1, keepdims=True)
            p_round = probs.astype(BF16)
            att_s[mine, cb] = unstack(dot(p_round, vt)).astype(BF16)
            p_grad = dot_t(a2, vt)
            s_grad = probs * (p_grad - jnp.sum(probs * p_grad, axis=-1, keepdims=True)) * factor
            s_grad = s_grad.astype(BF16)
            vgr_s[other, cb] = t_dot(p_round, a2).astype(BF16)
            q_backs[s] = unstack(dot(s_grad, kt))
            k_backs[1 - s] = t_dot(s_grad, q2)
        q_back = jnp.concatenate(q_backs, axis=0)
        k_back = jnp.concatenate(k_backs, axis=0)
        qg_s[:, cb] = ((q_back - q_unit * head_mean(q_back * q_unit)) * q_inv).astype(BF16)
        kg_s[:, cb] = ((k_back - k_unit * head_mean(k_back * k_unit)) * k_inv).astype(BF16)

    decoded = (views_f + dot(att_s[...], w[3])).astype(BF16)
    dec_ref[...] = decoded.reshape(sides, tokens, cols)
    view_term = cot.astype(F32) + dot_t(qg_s[...], w[0])
    norm_grad = dot_t(kg_s[...], w[1]) + dot_t(vgr_s[...], w[2])
    context_term = (
        norm_grad
        - jnp.mean(norm_grad, axis=-1, keepdims=True)
        - y_hat * jnp.mean(norm_grad * y_hat, axis=-1, keepdims=True)
    ) * inv_std
    vg_ref[...] = (view_term + context_term).astype(BF16).reshape(sides, tokens, cols)


def whole_kernel(
    wide, narrow, chunks, enc_ref, rows_ref, slot_ref, pick_ref, at_ref, order_ref, sums_ref,
    scale_ref, cot_ref, dec_ref, out_ref,
    send, recv, bcast_send, bcast_recv, local, wy, wz, stage, x_s, dec_s, vg_s, w, *rest,
):
    here = Place(wide, narrow)
    copies = Copies(send, recv)
    _, rows, cols = enc_ref.shape
    math, rest = rest[:8], rest[8:]

    def pick(owner, group):
        return pick_ref[group * wide + owner]

    def view_at(owner):
        return at_ref[owner]

    parts = []
    for i, (kind, lo, width) in enumerate(chunks):
        parts.append(Chunk(here, copies, kind, lo, width, pick, view_at, rest[8 * i:8 * i + 8]))
    a, b1, b2 = parts
    weights = Weights(here, copies, rows_ref, wy, wz, bcast_send, bcast_recv)

    here.barrier()
    b1.gather_first(enc_ref)
    a.gather_first(enc_ref)
    b2.gather_first(enc_ref)
    weights.start()
    a.gather_second()
    b1.gather_second()
    weights.second_y()
    b2.gather_second()
    along_y = weights.rounds_y()
    next(along_y)
    along_x = weights.rounds_z()
    next(along_x)
    b1.gather_third(slot_ref, stage, x_s, rows)
    next(along_y)
    b2.gather_third(slot_ref, stage, x_s, rows)
    next(along_x)
    next(along_y)
    a.gather_third(slot_ref, stage, x_s, rows)
    for _ in along_x:
        pass
    for _ in along_y:
        pass
    weights.finish()
    order_weights(wy, wz, order_ref, w)
    cot = cot_ref[...].reshape(2 * narrow * rows, cols)
    math[3][...] = dot_t(cot, w[3]).astype(BF16)
    for part in parts:
        part.back[2 * narrow] = jnp.zeros(part.back.shape[1:], BF16)
        part.wait()

    pair_pass(x_s, w, sums_ref, scale_ref, cot_ref, dec_s, vg_s, *math)
    save = pltpu.make_async_copy(dec_s, dec_ref, local)
    save.start()

    a.scatter_first(vg_s, rows)
    b1.scatter_first(vg_s, rows)
    b2.scatter_first(vg_s, rows)
    a.scatter_second()
    b1.scatter_second()
    b2.scatter_second()
    b1.scatter_third()
    a.scatter_third()
    b2.scatter_third()
    b1.scatter_end(out_ref)
    a.scatter_end(out_ref)
    b2.scatter_end(out_ref)
    copies.finish()
    save.wait()


def whole_call(wide, narrow, enc, weight_rows, slots, picks, view_at, head_scale, cot):
    zs, xs = wide // (X_SIZE * CORES), X_SIZE
    _, rows, cols = enc.shape
    heads = head_scale.shape[0]
    third = cols // 3
    chunks = (("x first", 0, third), ("z first", third, third), ("z first", 2 * third, third))
    views, tokens = 2 * narrow, narrow * rows
    wrows = weight_rows.shape[0]
    owners = 4
    order = jnp.asarray(order_rows(owners, wrows // 4, 4), BF16)
    sums = jnp.asarray(head_sums(2 * cols // heads), BF16)
    n_copies = 3 * 2 * (narrow - 1) + 2 * (3 * (zs + xs) + CORES * (zs + 2 * xs))
    n_copies += 3 * (zs + xs + narrow)
    smem = pl.BlockSpec(memory_space=pltpu.SMEM)
    vmem = pl.BlockSpec(memory_space=pltpu.VMEM)
    side = (2, tokens, cols)
    flat = (2 * tokens, cols)
    scratch = [
        pltpu.SemaphoreType.DMA((n_copies,)),
        pltpu.SemaphoreType.DMA((n_copies,)),
        pltpu.SemaphoreType.DMA((zs - 1,)),
        pltpu.SemaphoreType.DMA,
        pltpu.SemaphoreType.DMA,
        pltpu.VMEM((narrow, CORES, xs, wrows, cols // 2), BF16),
        pltpu.VMEM((CORES, xs, zs, wrows, cols // 2), BF16),
        pltpu.VMEM((views, rows, cols), BF16),
        pltpu.VMEM(side, BF16),
        pltpu.VMEM(side, BF16),
        pltpu.VMEM(side, BF16),
        pltpu.VMEM((4, cols, cols), BF16),
        pltpu.VMEM(flat, F32),
        pltpu.VMEM(flat, F32),
    ] + [pltpu.VMEM(flat, BF16)] * 6
    for kind, _, width in chunks:
        scratch += [pltpu.VMEM(s, BF16) for s in Chunk.shapes(kind, zs, xs, views, rows, width)]
    return pl.pallas_call(
        functools.partial(whole_kernel, wide, narrow, chunks),
        out_shape=(jax.ShapeDtypeStruct(side, BF16), jax.ShapeDtypeStruct(enc.shape, BF16)),
        in_specs=[vmem, vmem, smem, smem, smem, vmem, vmem, smem, vmem],
        out_specs=(pl.BlockSpec(memory_space=pl.ANY), vmem),
        scratch_shapes=scratch,
        compiler_params=pltpu.CompilerParams(
            collective_id=0, has_side_effects=True, vmem_limit_bytes=56 * 2**20
        ),
        name="whole",
    )(enc, weight_rows, slots, picks, view_at, order, sums, head_scale, cot)


def per_device(encodings, image_slot, pairs, attn_weights, head_scale, cotangent):
    wide = lax.axis_size("wide")
    narrow = lax.axis_size("narrow")
    images = image_slot.shape[0]
    views = 2 * narrow
    every = jnp.arange(images, dtype=jnp.int32)
    owners = jnp.arange(wide, dtype=jnp.int32)
    slots = jnp.sum(
        jnp.where(pairs[:, :, None] == every[None, None, :], image_slot[None, None, :], 0), axis=2
    ).reshape(wide, views)
    own = lax.dynamic_slice_in_dim(slots, lax.axis_index("wide"), 1, 0)[0]
    hits = slots[:, :, None] // 2 == owners[None, None, :]
    picks = jnp.sum(jnp.where(hits, slots[:, :, None] % 2, 0), axis=1).reshape(wide * wide)
    view = jnp.arange(views, dtype=jnp.int32)[:, None]
    view_at = views + jnp.sum(jnp.where(own[:, None] // 2 == owners[None, :], view - views, 0), axis=0)
    mats, wrows, cols = attn_weights.shape
    wpk = attn_weights.reshape(mats * wrows, cols)
    decoded, encoding_gradient = whole_call(
        wide, narrow, encodings, wpk, own, picks, view_at, head_scale, cotangent[0]
    )
    return (decoded[None], encoding_gradient)


def solution(mesh):
    return jax.shard_map(
        per_device,
        mesh=mesh,
        in_specs=(
            P("wide", "narrow", None),
            P(),
            P(),
            P(None, "wide", None),
            P(),
            P(("wide", "narrow"), None, None, None),
        ),
        out_specs=(P(("wide", "narrow"), None, None, None), P("wide", "narrow", None)),
        check_vma=False,
    )
```

time: 254 us -> 114 us (0.45)
  waiting for transfers between devices: 116 us -> 0 us
  Pallas kernels: 0 us -> 105 us
  local copies, waits for them, and re-layouts: 52.1 us -> 5.58 us
  starting transfers between devices: 34.6 us -> 0 us
  matrix products: 33.2 us -> 0 us
  between operations: 14.5 us -> 0.7 us
    all_to_all x4 -> x0, waiting for transfers between devices: 105 us -> none  [the longest x1 41.7 us: per_device(): lax.all_to_all(outgoing, 'wide', split_axis=0, concat_axis=0, tiled=True)]
    pallas_call x0 -> x1, Pallas kernels: none -> 105 us  [whole_call(): pl.pallas_call(functools.partial(whole_kernel, wide, narrow, chunks), out...]
    all_to_all x4 -> x0, starting transfers between devices: 34.5 us -> none  [the longest x1 14.8 us: per_device(): lax.all_to_all(outgoing, 'wide', split_axis=0, concat_axis=0, tiled=True)]
    dot_general x16 -> x0, matrix products: 30 us -> none  [the longest x1 4.89 us: pair_pass(): jnp.einsum('shqk,sqhd->skhd', score_grad, query_round, preferred_element_...]
    slice x1 -> x0, local copies, waits for them, and re-layouts: 15.8 us -> none  [pair_pass(): value_proj = jnp.dot(y_norm, weights[2], preferred_element_type=jnp.float32)]
    dot_general x2 -> x0, local copies, waits for them, and re-layouts: 10.9 us -> none  [the longest x1 6.42 us: pair_pass(): jnp.dot(flat_views, weights[0], preferred_element_type=jnp.float32)]
    convert_element_type x9 -> x0, local copies, waits for them, and re-layouts: 10.6 us -> none  [the longest x1 2.04 us: per_device(): outgoing = jnp.einsum('hk,krd->hrd', choose, encodings, preferred_element...]
    all_gather x1 -> x0, waiting for transfers between devices: 10 us -> none  [per_device(): weights = lax.all_gather(attn_weights, 'wide', axis=1, tiled=True)]
  transfers between devices with their start and end apart: 5 -> 0, of which waited for: 5 -> 0; matrix products, arithmetic and copies ran while one was open for 6% -> 0% of each run, Pallas kernels for 0% -> 0%
where the time goes in v2:
time: 114 us; the launch traced here: 113 us
  Pallas kernels  105 us (92%)
  local copies, waits for them, and re-layouts  5.58 us (5%)
  other arithmetic  1.94 us (2%)
    pallas_call x1, Pallas kernels, whole_call(): pl.pallas_call(functools.partial(whole_kernel, wide, narrow, chunks), out...  105 us
    unnamed x9, local copies, waits for them, and re-layouts  3.98 us

profile of v2, /device:TPU:1, one launch (start us, length us, event | category | flops | bytes accessed | tf_op | source)
XLA Modules:
  0.0 113.3 jit_solution(5767045852926028447)
XLA Ops:
  0.6 0.0 copy-start.1
  0.6 0.0 copy-start.2
  0.7 0.7 copy-done.1
  1.3 0.0 copy-done.2
  1.3 0.4 select_reduce_fusion.1
  1.7 0.9 copy.14
  2.6 0.7 reshape.166.rows_ref
  3.3 0.1 copy.15
  3.4 0.1 reshape.167
  3.5 0.5 and_select_fusion
  4.1 0.1 select_reduce_fusion.2
  4.2 0.6 broadcast_add_fusion.at_ref
  4.8 0.3 select_reduce_fusion
  5.1 0.7 reshape.168.pick_ref
  5.8 105.1 %whole.1 = (bf16[2,128,768]{2,1,0:T(8,128)(2,1)}, bf16[2,16,768]{2,1,0:T(8,128)(2,1)}) custom-call(bf16[2,16,768]{2,1,0:T(8,128)(2,1)} %enc_ref.1, bf16[48,768]{1,0:T(8,128)(2,1)} %reshape.166.rows_ref, s32[16]{0:T(128)} %get-tuple-element.7.slot_ref, s32[4096]{0:T(1024)} %reshape.168.pick_ref, s32[64]{0:T(128)} %broadcast_add_fusion.at_ref, ...), custom_call_target="tpu_custom_call" | custom-call | tf_op jit(solution)/shard_map/whole/pallas_call | solution.py:593
  110.9 0.0 copy-start
  110.9 1.8 %copy.18 = bf16[1,2,128,768]{3,2,1,0:T(8,128)(2,1)} copy(bf16[1,2,128,768]{3,2,1,0:T(8,128)(2,1)} %bitcast.6) | data formatting | bytes 786432
  112.7 0.0 copy-done
  112.7 0.6 copy.19
  (1 shorter events, 0.0 us)
Async XLA Ops:
  0.6 0.7 copy-start.1
  0.6 0.7 copy-start.2
  110.9 1.8 %copy-start = (bf16[2,16,768]{2,1,0:T(8,128)(2,1)S(1)}, bf16[2,16,768]{2,1,0:T(8,128)(2,1)}, u32[]{:S(2)}) copy-start(bf16[2,16,768]{2,1,0:T(8,128)(2,1)} %get-tuple-element.14) | copy-start | bytes 147460

commit v3 on v2

--- a/solution.py
+++ b/solution.py
@@ -12,6 +12,7 @@
 BF16 = jnp.bfloat16
 F32 = jnp.float32
 X_SIZE = 4
+SCHEDULE = ("wy a1 b1 c1 wz a2 wyx b2 y c2 y y b3 x y y c3 x y x y a3").split()
 CORES = 2
 
 
@@ -72,55 +73,75 @@
 
 class Copies:
     def __init__(self, send, recv):
-        self.send, self.recv, self.made = send, recv, []
+        self.send, self.recv, self.groups = send, recv, []
+
+    def group(self, whole):
+        made = Group(self.send.at[len(self.groups)], self.recv.at[len(self.groups)], whole)
+        self.groups.append(made)
+        return made
 
     def start(self, src, dst, device):
-        k = len(self.made)
-        copy = pltpu.make_async_remote_copy(
+        made = self.group(dst)
+        made.start(src, dst, device)
+        return made
+
+    def finish(self):
+        for made in self.groups:
+            if made.everywhere:
+                made.wait_send()
+
+
+class Group:
+    everywhere = True
+
+    def __init__(self, send, recv, whole):
+        self.send, self.recv, self.whole = send, recv, whole
+
+    def start(self, src, dst, device):
+        pltpu.make_async_remote_copy(
             src_ref=src,
             dst_ref=dst,
-            send_sem=self.send.at[k],
-            recv_sem=self.recv.at[k],
+            send_sem=self.send,
+            recv_sem=self.recv,
             device_id=device,
             device_id_type=MESH,
-        )
-        copy.start()
-        self.made.append(copy)
-        return copy
-
-    def finish(self):
-        for copy in self.made:
-            copy.wait_send()
-
-
-def ring_gather(copies, size, pos, device, block, half, own=None, landed=None):
+        ).start()
+
+    def wait_send(self):
+        pltpu.make_async_copy(self.whole, self.whole, self.send).wait()
+
+    def wait_recv(self):
+        pltpu.make_async_copy(self.whole, self.whole, self.recv).wait()
+
+
+def ring_gather(copies, size, pos, device, piece, pieces, landed):
     plus, minus = device(lax.rem(pos + 1, size)), device(lax.rem(pos + size - 1, size))
-    first = block(pos) if own is None else own
-    up = copies.start(first, block(pos), plus)
-    down = copies.start(first, block(pos), minus)
-    if landed is not None:
-        landed(pos)
-    for t in range(1, size // 2):
-        yield
+    mid = size // 2
+    half = pieces // 2
+
+    def send(p, i, to):
+        return copies.start(piece(p, i), piece(p, i), to)
+
+    up = {i: send(pos, i, plus) for i in range(pieces)}
+    down = {i: send(pos, i, minus) for i in reversed(range(pieces))}
+    landed(pos)
+    for t in range(1, mid):
         left, right = lax.rem(pos + size - t, size), lax.rem(pos + t, size)
-        up.wait_recv()
-        if t < size // 2 - 1:
-            up = copies.start(block(left), block(left), plus)
-        else:
-            up = copies.start(half(left, 0), half(left, 0), plus)
-        down.wait_recv()
-        if t < size // 2 - 1:
-            down = copies.start(block(right), block(right), minus)
-        else:
-            down = copies.start(half(right, 1), half(right, 1), minus)
-        if landed is not None:
-            landed(left)
-            landed(right)
+        for i in range(pieces):
+            yield
+            j = pieces - 1 - i
+            up.pop(i).wait_recv()
+            if t < mid - 1 or i < half:
+                up[i] = send(left, i, plus)
+            down.pop(j).wait_recv()
+            if t < mid - 1 or j >= half:
+                down[j] = send(right, j, minus)
+        landed(left)
+        landed(right)
     yield
-    up.wait_recv()
-    down.wait_recv()
-    if landed is not None:
-        landed(lax.rem(pos + size // 2, size))
+    for made in list(up.values()) + list(down.values()):
+        made.wait_recv()
+    landed(lax.rem(pos + mid, size))
 
 
 class Chunk:
@@ -138,7 +159,7 @@
     def shapes(kind, zs, xs, views, rows, width):
         size1, size2 = (xs, zs) if kind == "x first" else (zs, xs)
         ends = (size1, 2, rows, width)
-        routed = (size2, CORES, size1, rows, width)
+        routed = (size2 * CORES, size1, rows, width)
         return [ends, routed, routed, (views + 1, rows, width), routed, routed, ends, ends]
 
     def wide(self, i1, i2, core):
@@ -152,33 +173,30 @@
         return [(s, lax.rem(self.at2 + s, self.size2)) for s in outward(self.size2) + [0]]
 
     def route(self, outgoing, incoming, block):
-        c, started = self.here.c, []
+        c = self.here.c
+        mine = self.at2 * CORES + c
+        self.started = self.copies.group(incoming.at[pl.ds(0, self.size2 * CORES - 1)])
         for s, p in self.second_places():
             for core in range(CORES):
                 for i in range(self.size1):
-                    outgoing[p, core, i] = block(i, p, core)
+                    outgoing[p * CORES + core, i] = block(i, p, core)
             for core in (c, 1 - c) if s else (1 - c,):
-                started.append(
-                    self.copies.start(
-                        outgoing.at[p, core], incoming.at[self.at2, c], self.target(p, core)
-                    )
+                self.started.start(
+                    outgoing.at[p * CORES + core], incoming.at[mine], self.target(p, core)
                 )
             if s == 0:
-                incoming[self.at2, c] = outgoing[self.at2, c]
-        return started
+                incoming[mine] = outgoing[mine]
 
     def gather_first(self, enc_ref):
-        self.started = [
-            self.copies.start(
+        self.started = self.copies.group(self.near.at[pl.ds(0, self.size1 - 1)])
+        for s in outward(self.size1):
+            self.started.start(
                 enc_ref.at[:, :, self.cols], self.near.at[self.at1], self.here.ring(self.axes[0], s)
             )
-            for s in outward(self.size1)
-        ]
         self.near[self.at1] = enc_ref[:, :, self.lo:self.hi]
 
     def gather_second(self):
-        for copy in self.started:
-            copy.wait_recv()
+        self.wait()
         c = self.here.c
 
         def chosen(i, p, core):
@@ -186,43 +204,37 @@
             group = self.wide(self.at1, p, core)
             return self.near[i, self.pick(owner, group)]
 
-        self.started = self.route(self.out2, self.in2, chosen)
+        self.route(self.out2, self.in2, chosen)
 
     def gather_third(self, slot_ref, stage, views_ref, rows):
-        for copy in self.started:
-            copy.wait_recv()
+        self.wait()
         here, n = self.here, self.here.n
         for v in range(2 * here.ys):
             owner = slot_ref[v] // 2
             oc, ox, oz = lax.rem(owner, CORES), lax.rem(owner // CORES, here.xs), owner // (CORES * here.xs)
             o1, o2 = (ox, oz) if self.axes[0] == "x" else (oz, ox)
-            stage[v, :, self.lo:self.hi] = self.in2[o2, oc, o1]
+            stage[v, :, self.lo:self.hi] = self.in2[o2 * CORES + oc, o1]
         mine = pl.ds(pl.multiple_of(n * rows, rows), rows)
-        self.started = []
+        self.started = self.copies.group(stage.at[pl.ds(0, 2 * (here.ys - 1)), :, self.cols])
         for s in outward(here.ys):
             m = lax.rem(n + s, here.ys)
-            self.started.append(
-                self.copies.start(
-                    stage.at[pl.ds(2 * m, 2), :, self.cols], views_ref.at[:, mine, self.cols], here.at(n=m)
-                )
+            self.started.start(
+                stage.at[pl.ds(2 * m, 2), :, self.cols], views_ref.at[:, mine, self.cols], here.at(n=m)
             )
         for side in range(2):
             views_ref[side, mine, self.lo:self.hi] = stage[2 * n + side, :, self.lo:self.hi]
 
     def wait(self):
-        for copy in self.started:
-            copy.wait_recv()
+        self.started.wait_recv()
 
     def scatter_first(self, grad_ref, rows):
         here, n = self.here, self.here.n
         mine = pl.ds(2 * n, 2)
-        self.started = []
+        self.started = self.copies.group(self.back.at[pl.ds(0, 2 * (here.ys - 1))])
         for s in outward(here.ys):
             m = lax.rem(n + s, here.ys)
             theirs = pl.ds(pl.multiple_of(m * rows, rows), rows)
-            self.started.append(
-                self.copies.start(grad_ref.at[:, theirs, self.cols], self.back.at[mine], here.at(n=m))
-            )
+            self.started.start(grad_ref.at[:, theirs, self.cols], self.back.at[mine], here.at(n=m))
         own = pl.ds(pl.multiple_of(n * rows, rows), rows)
         for side in range(2):
             self.back[2 * n + side] = grad_ref[side, own, self.lo:self.hi]
@@ -233,19 +245,19 @@
         def term(i, p, core):
             return self.back[self.view_at(self.wide(i, p, core))]
 
-        self.started = self.route(self.bout2, self.bin2, term)
+        self.route(self.bout2, self.bin2, term)
 
     def scatter_third(self):
         self.wait()
         here, c = self.here, self.here.c
-        self.started = []
+        self.started = self.copies.group(self.last.at[pl.ds(0, self.size1 - 1)])
         for s in outward(self.size1) + [0]:
             i = lax.rem(self.at1 + s, self.size1)
-            totals = [jnp.zeros(self.bin2.shape[3:], F32)] * 2
+            totals = [jnp.zeros(self.bin2.shape[2:], F32)] * 2
             owner = self.wide(i, self.at2, c)
             for p in range(self.size2):
                 for core in range(CORES):
-                    block = self.bin2[p, core, i].astype(F32)
+                    block = self.bin2[p * CORES + core, i].astype(F32)
                     image = self.pick(owner, self.wide(self.at1, p, core))
                     totals[0] = totals[0] + jnp.where(image == 0, block, 0.0)
                     totals[1] = totals[1] + jnp.where(image == 0, 0.0, block)
@@ -254,11 +266,7 @@
                 continue
             for k in range(2):
                 self.sums[i, k] = totals[k].astype(BF16)
-            self.started.append(
-                self.copies.start(
-                    self.sums.at[i], self.last.at[self.at1], here.ring(self.axes[0], s)
-                )
-            )
+            self.started.start(self.sums.at[i], self.last.at[self.at1], here.ring(self.axes[0], s))
 
     def scatter_end(self, out_ref):
         self.wait()
@@ -270,97 +278,88 @@
 
 
 class Weights:
-    def __init__(self, here, copies, rows_ref, wy, wz, bcast_send, bcast_recv):
+    def __init__(self, here, copies, rows_ref, wy, wz):
         self.here, self.copies = here, copies
         self.half = rows_ref.shape[1] // 2
         self.src_y = rows_ref.at[:, pl.ds(0, self.half)]
         self.src_z = rows_ref.at[:, pl.ds(self.half, self.half)]
         self.rows_ref, self.wy, self.wz = rows_ref, wy, wz
-        self.bcast_send, self.bcast_recv = bcast_send, bcast_recv
-        self.passed = []
-
-    def from_z(self, s):
+
+    def start_y(self):
         here = self.here
-        return pltpu.make_async_remote_copy(
-            src_ref=self.src_y,
-            dst_ref=self.wy.at[here.n, here.c, here.x],
-            send_sem=self.bcast_send.at[s - 1],
-            recv_sem=self.bcast_recv,
-            device_id=here.ring("z", s),
-            device_id_type=MESH,
-        )
-
-    def start(self):
-        here, copies = self.here, self.copies
+        self.from_z = self.copies.group(self.wz.at[0, 0, pl.ds(0, here.zs - 1)])
+        self.from_z.everywhere = False
 
         @pl.when(here.z == here.n)
         def _():
             for s in outward(here.zs):
-                self.from_z(s).start()
+                self.from_z.start(self.src_y, self.wy.at[here.n, here.c, here.x], here.ring("z", s))
             self.wy[here.n, here.c, here.x] = self.rows_ref[:, :self.half]
 
-        self.along_z = [
-            copies.start(self.src_z, self.wz.at[here.c, here.x, here.z], here.ring("z", s))
-            for s in outward(here.zs)
-        ]
+    def start_z(self):
+        here = self.here
+        self.along_z = self.copies.group(self.wz.at[0, 0, pl.ds(0, here.zs - 1)])
+        for s in outward(here.zs):
+            self.along_z.start(self.src_z, self.wz.at[here.c, here.x, here.z], here.ring("z", s))
         self.wz[here.c, here.x, here.z] = self.rows_ref[:, self.half:]
 
     def second_y(self):
         here = self.here
+        block = self.wy.at[here.n, here.c, here.x]
 
         @pl.when(here.z != here.n)
         def _():
-            self.from_z(1).wait_recv()
-
-        block = self.wy.at[here.n, here.c, here.x]
-        self.along_x = [self.copies.start(block, block, here.ring("x", s)) for s in outward(here.xs)]
+            pltpu.make_async_copy(block, block, self.from_z.recv).wait()
+
+        self.along_x = self.copies.group(self.wy.at[0, 0, pl.ds(0, here.xs - 1)])
+        for s in outward(here.xs):
+            self.along_x.start(block, block, here.ring("x", s))
 
     def rounds_y(self):
-        here, copies = self.here, self.copies
-        for copy in self.along_x:
-            copy.wait_recv()
-
-        def block(p):
-            return self.wy.at[p, here.c]
-
-        def half(p, h):
-            return self.wy.at[p, here.c, pl.ds(h * (here.xs // 2), here.xs // 2)]
+        here = self.here
+        self.along_x.wait_recv()
+        self.passed_y = self.copies.group(self.wy.at[:, 0])
+        pieces = 2
+        size = here.xs // pieces
+
+        def piece(p, i):
+            return self.wy.at[p, here.c, pl.ds(i * size, size)]
 
         yield from ring_gather(
-            copies, here.ys, here.n, lambda p: here.at(n=p), block, half, landed=self.hand_on(block)
+            self.copies, here.ys, here.n, lambda p: here.at(n=p), piece, pieces,
+            self.hand_on(self.passed_y, lambda p: self.wy.at[p, here.c]),
         )
 
     def rounds_z(self):
-        here, copies = self.here, self.copies
-        for copy in self.along_z:
-            copy.wait_recv()
-
-        def block(p):
-            return self.wz.at[here.c, p]
-
-        def half(p, h):
-            return self.wz.at[here.c, p, pl.ds(h * (here.zs // 2), here.zs // 2)]
+        here = self.here
+        self.along_z.wait_recv()
+        self.passed_z = self.copies.group(self.wz.at[0])
+        pieces = 2
+        size = here.zs // pieces
+
+        def piece(p, i):
+            return self.wz.at[here.c, p, pl.ds(i * size, size)]
 
         yield from ring_gather(
-            copies, here.xs, here.x, lambda p: here.at(x=p), block, half, landed=self.hand_on(block)
+            self.copies, here.xs, here.x, lambda p: here.at(x=p), piece, pieces,
+            self.hand_on(self.passed_z, lambda p: self.wz.at[here.c, p]),
         )
 
-    def hand_on(self, block):
+    def hand_on(self, group, block):
         sibling = self.here.at(c=1 - self.here.c)
 
         def landed(p):
-            self.passed.append(self.copies.start(block(p), block(p), sibling))
+            group.start(block(p), block(p), sibling)
 
         return landed
 
     def finish(self):
-        for copy in self.passed:
-            copy.wait_recv()
+        self.passed_y.wait_recv()
+        self.passed_z.wait_recv()
 
         @pl.when(self.here.z == self.here.n)
         def _():
-            for s in outward(self.here.zs):
-                self.from_z(s).wait_send()
+            self.from_z.wait_send()
 
 
 def order_rows(owners, per_owner, mats):
@@ -483,9 +482,9 @@
 
 
 def whole_kernel(
-    wide, narrow, chunks, enc_ref, rows_ref, slot_ref, pick_ref, at_ref, order_ref, sums_ref,
+    wide, narrow, chunks, enc_ref, mats_ref, slot_ref, pick_ref, at_ref, order_ref, sums_ref,
     scale_ref, cot_ref, dec_ref, out_ref,
-    send, recv, bcast_send, bcast_recv, local, wy, wz, stage, x_s, dec_s, vg_s, w, *rest,
+    send, recv, local, rows_s, wy, wz, stage, x_s, dec_s, vg_s, w, *rest,
 ):
     here = Place(wide, narrow)
     copies = Copies(send, recv)
@@ -502,27 +501,27 @@
     for i, (kind, lo, width) in enumerate(chunks):
         parts.append(Chunk(here, copies, kind, lo, width, pick, view_at, rest[8 * i:8 * i + 8]))
     a, b1, b2 = parts
-    weights = Weights(here, copies, rows_ref, wy, wz, bcast_send, bcast_recv)
+    weights = Weights(here, copies, rows_s, wy, wz)
+    rows_s[...] = jnp.concatenate(
+        [mats_ref[i].astype(F32) for i in range(mats_ref.shape[0])], axis=0
+    ).astype(BF16)
 
     here.barrier()
-    b1.gather_first(enc_ref)
-    a.gather_first(enc_ref)
-    b2.gather_first(enc_ref)
-    weights.start()
-    a.gather_second()
-    b1.gather_second()
-    weights.second_y()
-    b2.gather_second()
     along_y = weights.rounds_y()
-    next(along_y)
     along_x = weights.rounds_z()
-    next(along_x)
-    b1.gather_third(slot_ref, stage, x_s, rows)
-    next(along_y)
-    b2.gather_third(slot_ref, stage, x_s, rows)
-    next(along_x)
-    next(along_y)
-    a.gather_third(slot_ref, stage, x_s, rows)
+    steps = {
+        "wy": weights.start_y,
+        "wz": weights.start_z,
+        "wyx": weights.second_y,
+        "y": lambda: next(along_y, None),
+        "x": lambda: next(along_x, None),
+    }
+    for name, part in (("a", a), ("b", b1), ("c", b2)):
+        steps[name + "1"] = functools.partial(part.gather_first, enc_ref)
+        steps[name + "2"] = part.gather_second
+        steps[name + "3"] = functools.partial(part.gather_third, slot_ref, stage, x_s, rows)
+    for step in SCHEDULE:
+        steps[step]()
     for _ in along_x:
         pass
     for _ in along_y:
@@ -551,33 +550,32 @@
     b1.scatter_end(out_ref)
     a.scatter_end(out_ref)
     b2.scatter_end(out_ref)
+    assert len(copies.groups) < send.shape[0], len(copies.groups)
     copies.finish()
     save.wait()
 
 
-def whole_call(wide, narrow, enc, weight_rows, slots, picks, view_at, head_scale, cot):
+def whole_call(wide, narrow, enc, weight_mats, slots, picks, view_at, head_scale, cot):
     zs, xs = wide // (X_SIZE * CORES), X_SIZE
     _, rows, cols = enc.shape
     heads = head_scale.shape[0]
     third = cols // 3
     chunks = (("x first", 0, third), ("z first", third, third), ("z first", 2 * third, third))
     views, tokens = 2 * narrow, narrow * rows
-    wrows = weight_rows.shape[0]
+    wrows = weight_mats.shape[0] * weight_mats.shape[1]
     owners = 4
     order = jnp.asarray(order_rows(owners, wrows // 4, 4), BF16)
     sums = jnp.asarray(head_sums(2 * cols // heads), BF16)
-    n_copies = 3 * 2 * (narrow - 1) + 2 * (3 * (zs + xs) + CORES * (zs + 2 * xs))
-    n_copies += 3 * (zs + xs + narrow)
+    n_groups = 18 + 5 + 2 * 3 * (narrow // 2 + X_SIZE // 2 - 2) + 4
     smem = pl.BlockSpec(memory_space=pltpu.SMEM)
     vmem = pl.BlockSpec(memory_space=pltpu.VMEM)
     side = (2, tokens, cols)
     flat = (2 * tokens, cols)
     scratch = [
-        pltpu.SemaphoreType.DMA((n_copies,)),
-        pltpu.SemaphoreType.DMA((n_copies,)),
-        pltpu.SemaphoreType.DMA((zs - 1,)),
+        pltpu.SemaphoreType.DMA((n_groups,)),
+        pltpu.SemaphoreType.DMA((n_groups,)),
         pltpu.SemaphoreType.DMA,
-        pltpu.SemaphoreType.DMA,
+        pltpu.VMEM((wrows, cols), BF16),
         pltpu.VMEM((narrow, CORES, xs, wrows, cols // 2), BF16),
         pltpu.VMEM((CORES, xs, zs, wrows, cols // 2), BF16),
         pltpu.VMEM((views, rows, cols), BF16),
@@ -600,7 +598,7 @@
             collective_id=0, has_side_effects=True, vmem_limit_bytes=56 * 2**20
         ),
         name="whole",
-    )(enc, weight_rows, slots, picks, view_at, order, sums, head_scale, cot)
+    )(enc, weight_mats, slots, picks, view_at, order, sums, head_scale, cot)
 
 
 def per_device(encodings, image_slot, pairs, attn_weights, head_scale, cotangent):
@@ -618,10 +616,8 @@
     picks = jnp.sum(jnp.where(hits, slots[:, :, None] % 2, 0), axis=1).reshape(wide * wide)
     view = jnp.arange(views, dtype=jnp.int32)[:, None]
     view_at = views + jnp.sum(jnp.where(own[:, None] // 2 == owners[None, :], view - views, 0), axis=0)
-    mats, wrows, cols = attn_weights.shape
-    wpk = attn_weights.reshape(mats * wrows, cols)
     decoded, encoding_gradient = whole_call(
-        wide, narrow, encodings, wpk, own, picks, view_at, head_scale, cotangent[0]
+        wide, narrow, encodings, attn_weights, own, picks, view_at, head_scale, cotangent[0]
     )
     return (decoded[None], encoding_gradient)
 

time: 114 us -> 101 us (0.89)
  Pallas kernels: 105 us -> 92.7 us
    pallas_call x1, Pallas kernels: 105 us -> 92.7 us  [whole_call(): pl.pallas_call(functools.partial(whole_kernel, wide, narrow, chunks), out...]
where the time goes in v3:
time: 101 us
  Pallas kernels  92.7 us (92%)
  local copies, waits for them, and re-layouts  5.57 us (6%)
  other arithmetic  1.94 us (2%)
    pallas_call x1, Pallas kernels, whole_call(): pl.pallas_call(functools.partial(whole_kernel, wide, narrow, chunks), out...  92.7 us
    unnamed x9, local copies, waits for them, and re-layouts  4.62 us

profile of v3, /device:TPU:1, one launch (start us, length us, event | category | flops | bytes accessed | tf_op | source)
XLA Modules:
  0.0 100.9 jit_solution(18180253286901716507)
XLA Ops:
  0.6 0.0 copy-start.1
  0.6 0.0 copy-start.2
  0.7 0.7 copy-done.1
  1.3 0.0 copy-done.2
  1.3 0.4 select_reduce_fusion.1
  1.7 1.5 %copy.15.mats_ref = bf16[4,12,768]{2,1,0:T(8,128)(2,1)} copy(bf16[4,12,768]{2,0,1:T(4,128)(2,1)} %param.11) | data formatting | bytes 147456 | tf_op args[3]
  3.2 0.1 copy.14
  3.4 0.1 reshape.163
  3.5 0.5 and_select_fusion
  4.1 0.1 select_reduce_fusion.2
  4.1 0.6 broadcast_add_fusion.at_ref
  4.8 0.3 select_reduce_fusion
  5.1 0.7 reshape.164.pick_ref
  5.8 92.7 %whole.1 = (bf16[2,128,768]{2,1,0:T(8,128)(2,1)}, bf16[2,16,768]{2,1,0:T(8,128)(2,1)}) custom-call(bf16[2,16,768]{2,1,0:T(8,128)(2,1)} %enc_ref.1, bf16[4,12,768]{2,1,0:T(8,128)(2,1)} %copy.15.mats_ref, s32[16]{0:T(128)} %get-tuple-element.7.slot_ref, s32[4096]{0:T(1024)} %reshape.164.pick_ref, s32[64]{0:T(128)} %broadcast_add_fusion.at_ref, ...), custom_call_target="tpu_custom_call" | custom-call | tf_op jit(solution)/shard_map/whole/pallas_call | solution.py:591
  98.5 0.0 copy-start
  98.5 1.8 %copy.18 = bf16[1,2,128,768]{3,2,1,0:T(8,128)(2,1)} copy(bf16[1,2,128,768]{3,2,1,0:T(8,128)(2,1)} %bitcast.6) | data formatting | bytes 786432
  100.3 0.0 copy-done
  100.3 0.6 copy.19
  (1 shorter events, 0.0 us)
Async XLA Ops:
  0.6 0.7 copy-start.1
  0.6 0.7 copy-start.2
  98.5 1.8 %copy-start = (bf16[2,16,768]{2,1,0:T(8,128)(2,1)S(1)}, bf16[2,16,768]{2,1,0:T(8,128)(2,1)}, u32[]{:S(2)}) copy-start(bf16[2,16,768]{2,1,0:T(8,128)(2,1)} %get-tuple-element.14) | copy-start | bytes 147460

commit v4 on v3

--- a/solution.py
+++ b/solution.py
@@ -12,7 +12,13 @@
 BF16 = jnp.bfloat16
 F32 = jnp.float32
 X_SIZE = 4
-SCHEDULE = ("wy a1 b1 c1 wz a2 wyx b2 y c2 y y b3 x y y c3 x y x y a3").split()
+SCHEDULE = (
+    "wy", "a1", "b1", "c1", "wz", "a2", "wyx", "b2", "y", "c2", "y", "y", "b3", "x", "o", "y", "y",
+    "c3", "x", "o", "y", "x", "o", "y", "a3", "xs", "o", "o", "ys", "oz", "o", "o", "o",
+)
+Y_PIECES = 2
+X_PIECES = 2
+BACK = "abc"
 CORES = 2
 
 
@@ -206,11 +212,11 @@
 
         self.route(self.out2, self.in2, chosen)
 
-    def gather_third(self, slot_ref, stage, views_ref, rows):
+    def gather_third(self, owner_of, stage, views_ref, rows):
         self.wait()
         here, n = self.here, self.here.n
         for v in range(2 * here.ys):
-            owner = slot_ref[v] // 2
+            owner = owner_of(v)
             oc, ox, oz = lax.rem(owner, CORES), lax.rem(owner // CORES, here.xs), owner // (CORES * here.xs)
             o1, o2 = (ox, oz) if self.axes[0] == "x" else (oz, ox)
             stage[v, :, self.lo:self.hi] = self.in2[o2 * CORES + oc, o1]
@@ -229,7 +235,7 @@
 
     def scatter_first(self, grad_ref, rows):
         here, n = self.here, self.here.n
-        mine = pl.ds(2 * n, 2)
+        mine = pl.ds(2 * n + 1, 2)
         self.started = self.copies.group(self.back.at[pl.ds(0, 2 * (here.ys - 1))])
         for s in outward(here.ys):
             m = lax.rem(n + s, here.ys)
@@ -237,7 +243,7 @@
             self.started.start(grad_ref.at[:, theirs, self.cols], self.back.at[mine], here.at(n=m))
         own = pl.ds(pl.multiple_of(n * rows, rows), rows)
         for side in range(2):
-            self.back[2 * n + side] = grad_ref[side, own, self.lo:self.hi]
+            self.back[2 * n + 1 + side] = grad_ref[side, own, self.lo:self.hi]
 
     def scatter_second(self):
         self.wait()
@@ -318,45 +324,61 @@
     def rounds_y(self):
         here = self.here
         self.along_x.wait_recv()
-        self.passed_y = self.copies.group(self.wy.at[:, 0])
-        pieces = 2
-        size = here.xs // pieces
+        self.landed_y = []
+        size = here.xs // Y_PIECES
 
         def piece(p, i):
             return self.wy.at[p, here.c, pl.ds(i * size, size)]
 
+        def landed(p):
+            block = self.wy.at[p, here.c]
+            self.landed_y.append((p, self.copies.start(block, block, here.at(c=1 - here.c))))
+
         yield from ring_gather(
-            self.copies, here.ys, here.n, lambda p: here.at(n=p), piece, pieces,
-            self.hand_on(self.passed_y, lambda p: self.wy.at[p, here.c]),
+            self.copies, here.ys, here.n, lambda p: here.at(n=p), piece, Y_PIECES, landed
         )
 
     def rounds_z(self):
         here = self.here
         self.along_z.wait_recv()
         self.passed_z = self.copies.group(self.wz.at[0])
-        pieces = 2
-        size = here.zs // pieces
+        size = here.zs // X_PIECES
 
         def piece(p, i):
             return self.wz.at[here.c, p, pl.ds(i * size, size)]
 
+        def landed(p):
+            block = self.wz.at[here.c, p]
+            self.passed_z.start(block, block, here.at(c=1 - here.c))
+
         yield from ring_gather(
-            self.copies, here.xs, here.x, lambda p: here.at(x=p), piece, pieces,
-            self.hand_on(self.passed_z, lambda p: self.wz.at[here.c, p]),
+            self.copies, here.xs, here.x, lambda p: here.at(x=p), piece, X_PIECES, landed
         )
 
-    def hand_on(self, group, block):
-        sibling = self.here.at(c=1 - self.here.c)
-
-        def landed(p):
-            group.start(block(p), block(p), sibling)
-
-        return landed
+    def order(self, order, z, block, part, w):
+        here = self.here
+        mats = w.shape[0]
+        owners = order.shape[0] // self.rows_ref.shape[0]
+        count = order.shape[0] // mats
+        for q in range(here.xs * CORES // owners):
+            pieces = [block(o // CORES, o % CORES) for o in range(q * owners, (q + 1) * owners)]
+            ordered = dot(order, jnp.concatenate(pieces, axis=0)).astype(BF16)
+            at = z * (here.xs * CORES // owners) + q
+            rows = pl.ds(pl.multiple_of(at * count, count), count)
+            for i in range(mats):
+                w[i, rows, part * self.half:(part + 1) * self.half] = ordered[i * count:(i + 1) * count]
+
+    def order_y(self, order, w):
+        p, passed = self.landed_y.pop(0)
+        passed.wait_recv()
+        self.order(order[...], p, lambda x, c: self.wy[p, c, x], 0, w)
+
+    def order_z(self, order, w):
+        self.passed_z.wait_recv()
+        for z in range(self.here.zs):
+            self.order(order[...], z, lambda x, c: self.wz[c, x, z], 1, w)
 
     def finish(self):
-        self.passed_y.wait_recv()
-        self.passed_z.wait_recv()
-
         @pl.when(self.here.z == self.here.n)
         def _():
             self.from_z.wait_send()
@@ -368,7 +390,7 @@
     for i in range(mats):
         for o in range(owners):
             for r in range(per_owner):
-                table[(i * owners + o) * per_owner + r, (o * mats + i) * per_owner + r] = 1.0
+                table[(i * owners + o) * per_owner + r, (o * per_owner + r) * mats + i] = 1.0
     return table
 
 
@@ -377,25 +399,6 @@
     row = (np.arange(2 * width) % width) // half
     col = np.arange(width) // half
     return (row[:, None] == col[None, :]).astype(np.float32)
-
-
-def order_weights(wy, wz, order_ref, w):
-    zs, cores, xs, wrows, half = wy.shape
-    mats = w.shape[0]
-    order = order_ref[...]
-    owners = order.shape[0] // wrows
-    group_rows = order.shape[0] // mats
-    for q in range(zs * xs * cores // owners):
-        for part in range(2):
-            pieces = []
-            for o in range(q * owners, (q + 1) * owners):
-                oc, ox, oz = o % cores, (o // cores) % xs, o // (cores * xs)
-                pieces.append(wy[oz, oc, ox] if part == 0 else wz[oc, ox, oz])
-            ordered = dot(order, jnp.concatenate(pieces, axis=0)).astype(BF16)
-            for i in range(mats):
-                w[i, q * group_rows:(q + 1) * group_rows, part * half:(part + 1) * half] = (
-                    ordered[i * group_rows:(i + 1) * group_rows]
-                )
 
 
 def pair_pass(
@@ -482,9 +485,9 @@
 
 
 def whole_kernel(
-    wide, narrow, chunks, enc_ref, mats_ref, slot_ref, pick_ref, at_ref, order_ref, sums_ref,
-    scale_ref, cot_ref, dec_ref, out_ref,
-    send, recv, local, rows_s, wy, wz, stage, x_s, dec_s, vg_s, w, *rest,
+    wide, narrow, chunks, enc_ref, mats_ref, slot_ref, pairs_ref, table_ref, order_ref, sums_ref,
+    scale_ref, cot_hbm, dec_ref, out_ref,
+    send, recv, local, cot_ref, order_s, sums_s, rows_s, wy, wz, stage, x_s, dec_s, vg_s, w, *rest,
 ):
     here = Place(wide, narrow)
     copies = Copies(send, recv)
@@ -492,10 +495,13 @@
     math, rest = rest[:8], rest[8:]
 
     def pick(owner, group):
-        return pick_ref[group * wide + owner]
+        return lax.rem(table_ref[group, owner], 2)
 
     def view_at(owner):
-        return at_ref[owner]
+        return table_ref[here.w, owner] // 2
+
+    def owner_of(v):
+        return slot_ref[pairs_ref[v % 2, here.w * narrow + v // 2]] // 2
 
     parts = []
     for i, (kind, lo, width) in enumerate(chunks):
@@ -503,9 +509,15 @@
     a, b1, b2 = parts
     weights = Weights(here, copies, rows_s, wy, wz)
     rows_s[...] = jnp.concatenate(
-        [mats_ref[i].astype(F32) for i in range(mats_ref.shape[0])], axis=0
+        [mats_ref[r].astype(F32) for r in range(mats_ref.shape[0])], axis=0
     ).astype(BF16)
 
+    loads = [
+        pltpu.make_async_copy(src, dst, local.at[i])
+        for i, (src, dst) in enumerate(((order_ref, order_s), (sums_ref, sums_s), (cot_hbm, cot_ref)))
+    ]
+    for load in loads:
+        load.start()
     here.barrier()
     along_y = weights.rounds_y()
     along_x = weights.rounds_z()
@@ -515,47 +527,49 @@
         "wyx": weights.second_y,
         "y": lambda: next(along_y, None),
         "x": lambda: next(along_x, None),
+        "ys": lambda: list(along_y),
+        "xs": lambda: list(along_x),
+        "o": lambda: weights.order_y(order_s, w),
+        "oz": lambda: weights.order_z(order_s, w),
     }
     for name, part in (("a", a), ("b", b1), ("c", b2)):
         steps[name + "1"] = functools.partial(part.gather_first, enc_ref)
         steps[name + "2"] = part.gather_second
-        steps[name + "3"] = functools.partial(part.gather_third, slot_ref, stage, x_s, rows)
+        steps[name + "3"] = functools.partial(part.gather_third, owner_of, stage, x_s, rows)
+    ready = []
     for step in SCHEDULE:
+        if step == "o" and not ready:
+            for load in loads[:2]:
+                load.wait()
+            ready.append(True)
         steps[step]()
-    for _ in along_x:
-        pass
-    for _ in along_y:
-        pass
     weights.finish()
-    order_weights(wy, wz, order_ref, w)
+    loads[2].wait()
     cot = cot_ref[...].reshape(2 * narrow * rows, cols)
     math[3][...] = dot_t(cot, w[3]).astype(BF16)
     for part in parts:
-        part.back[2 * narrow] = jnp.zeros(part.back.shape[1:], BF16)
+        part.back[0] = jnp.zeros(part.back.shape[1:], BF16)
         part.wait()
 
-    pair_pass(x_s, w, sums_ref, scale_ref, cot_ref, dec_s, vg_s, *math)
-    save = pltpu.make_async_copy(dec_s, dec_ref, local)
+    pair_pass(x_s, w, sums_s, scale_ref, cot_ref, dec_s, vg_s, *math)
+    save = pltpu.make_async_copy(dec_s, dec_ref, local.at[3])
     save.start()
 
-    a.scatter_first(vg_s, rows)
-    b1.scatter_first(vg_s, rows)
-    b2.scatter_first(vg_s, rows)
-    a.scatter_second()
-    b1.scatter_second()
-    b2.scatter_second()
-    b1.scatter_third()
-    a.scatter_third()
-    b2.scatter_third()
-    b1.scatter_end(out_ref)
-    a.scatter_end(out_ref)
-    b2.scatter_end(out_ref)
-    assert len(copies.groups) < send.shape[0], len(copies.groups)
+    back = [parts["abc".index(name)] for name in BACK]
+    for part in back:
+        part.scatter_first(vg_s, rows)
+    for part in back:
+        part.scatter_second()
+    for part in parts:
+        part.scatter_third()
+    for part in parts:
+        part.scatter_end(out_ref)
+    assert len(copies.groups) == send.shape[0]
     copies.finish()
     save.wait()
 
 
-def whole_call(wide, narrow, enc, weight_mats, slots, picks, view_at, head_scale, cot):
+def whole_call(wide, narrow, enc, weight_mats, image_slot, pairs, table, head_scale, cot):
     zs, xs = wide // (X_SIZE * CORES), X_SIZE
     _, rows, cols = enc.shape
     heads = head_scale.shape[0]
@@ -566,7 +580,8 @@
     owners = 4
     order = jnp.asarray(order_rows(owners, wrows // 4, 4), BF16)
     sums = jnp.asarray(head_sums(2 * cols // heads), BF16)
-    n_groups = 18 + 5 + 2 * 3 * (narrow // 2 + X_SIZE // 2 - 2) + 4
+    n_groups = 18 + 4 + narrow + Y_PIECES * (narrow - 1) + X_PIECES * (X_SIZE - 1)
+    anywhere = pl.BlockSpec(memory_space=pl.ANY)
     smem = pl.BlockSpec(memory_space=pltpu.SMEM)
     vmem = pl.BlockSpec(memory_space=pltpu.VMEM)
     side = (2, tokens, cols)
@@ -574,7 +589,10 @@
     scratch = [
         pltpu.SemaphoreType.DMA((n_groups,)),
         pltpu.SemaphoreType.DMA((n_groups,)),
-        pltpu.SemaphoreType.DMA,
+        pltpu.SemaphoreType.DMA((4,)),
+        pltpu.VMEM(side, BF16),
+        pltpu.VMEM(order.shape, BF16),
+        pltpu.VMEM(sums.shape, BF16),
         pltpu.VMEM((wrows, cols), BF16),
         pltpu.VMEM((narrow, CORES, xs, wrows, cols // 2), BF16),
         pltpu.VMEM((CORES, xs, zs, wrows, cols // 2), BF16),
@@ -591,14 +609,14 @@
     return pl.pallas_call(
         functools.partial(whole_kernel, wide, narrow, chunks),
         out_shape=(jax.ShapeDtypeStruct(side, BF16), jax.ShapeDtypeStruct(enc.shape, BF16)),
-        in_specs=[vmem, vmem, smem, smem, smem, vmem, vmem, smem, vmem],
-        out_specs=(pl.BlockSpec(memory_space=pl.ANY), vmem),
+        in_specs=[vmem, vmem, smem, smem, smem, anywhere, anywhere, smem, anywhere],
+        out_specs=(anywhere, vmem),
         scratch_shapes=scratch,
         compiler_params=pltpu.CompilerParams(
             collective_id=0, has_side_effects=True, vmem_limit_bytes=56 * 2**20
         ),
         name="whole",
-    )(enc, weight_mats, slots, picks, view_at, order, sums, head_scale, cot)
+    )(enc, weight_mats, image_slot, pairs, table, order, sums, head_scale, cot)
 
 
 def per_device(encodings, image_slot, pairs, attn_weights, head_scale, cotangent):
@@ -611,13 +629,12 @@
     slots = jnp.sum(
         jnp.where(pairs[:, :, None] == every[None, None, :], image_slot[None, None, :], 0), axis=2
     ).reshape(wide, views)
-    own = lax.dynamic_slice_in_dim(slots, lax.axis_index("wide"), 1, 0)[0]
     hits = slots[:, :, None] // 2 == owners[None, None, :]
-    picks = jnp.sum(jnp.where(hits, slots[:, :, None] % 2, 0), axis=1).reshape(wide * wide)
-    view = jnp.arange(views, dtype=jnp.int32)[:, None]
-    view_at = views + jnp.sum(jnp.where(own[:, None] // 2 == owners[None, :], view - views, 0), axis=0)
+    view = jnp.arange(1, views + 1, dtype=jnp.int32)[None, :, None]
+    table = jnp.sum(jnp.where(hits, 2 * view + slots[:, :, None] % 2, 0), axis=1)
     decoded, encoding_gradient = whole_call(
-        wide, narrow, encodings, attn_weights, own, picks, view_at, head_scale, cotangent[0]
+        wide, narrow, encodings, attn_weights.transpose(1, 0, 2), image_slot, pairs.T, table,
+        head_scale, cotangent[0],
     )
     return (decoded[None], encoding_gradient)
 

time: 101 us -> 100 us (0.990)
  local copies, waits for them, and re-layouts: 5.57 us -> 3.35 us
  Pallas kernels: 92.7 us -> 94.5 us
    pallas_call x1, Pallas kernels: 92.7 us -> 94.5 us  [whole_call(): pl.pallas_call(functools.partial(whole_kernel, wide, narrow, chunks), out...]
    unnamed x9 -> x8, local copies, waits for them, and re-layouts: 4.62 us -> 3.07 us
where the time goes in v4:
time: 100 us
  Pallas kernels  94.5 us (94%)
  local copies, waits for them, and re-layouts  3.35 us (3%)
  other arithmetic  1.38 us (1%)
    pallas_call x1, Pallas kernels, whole_call(): pl.pallas_call(functools.partial(whole_kernel, wide, narrow, chunks), out...  94.5 us
    unnamed x8, local copies, waits for them, and re-layouts  3.07 us

profile of v4, /device:TPU:1, one launch (start us, length us, event | category | flops | bytes accessed | tf_op | source)
XLA Modules:
  0.0 100.0 jit_solution(10373359095872942430)
XLA Ops:
  0.6 0.0 copy-start.1
  0.6 0.0 copy-start.2
  0.7 0.7 copy-done.1
  1.3 0.0 copy-done.2
  1.3 0.4 select_reduce_fusion.1
  1.7 0.2 copy.12
  1.9 0.1 broadcast_in_dim_reshape.4
  2.0 1.0 select_reduce_fusion.table_ref
  3.0 94.5 %whole.1 = (bf16[2,128,768]{2,1,0:T(8,128)(2,1)}, bf16[2,16,768]{2,1,0:T(8,128)(2,1)}) custom-call(bf16[2,16,768]{2,1,0:T(8,128)(2,1)} %enc_ref.1, bf16[12,4,768]{2,1,0:T(4,128)(2,1)} %bitcast.6, s32[128]{0:T(128)} %slot_ref.1, s32[2,512]{1,0:T(2,128)} %bitcast.7, s32[64,64]{1,0:T(8,128)} %select_reduce_fusion.table_ref, ...), custom_call_target="tpu_custom_call" | custom-call | tf_op jit(solution)/shard_map/whole/pallas_call | solution.py:609
  97.6 0.0 copy-start
  97.6 1.8 %copy.15 = bf16[1,2,128,768]{3,2,1,0:T(8,128)(2,1)} copy(bf16[1,2,128,768]{3,2,1,0:T(8,128)(2,1)} %bitcast.4) | data formatting | bytes 786432
  99.3 0.0 copy-done
  99.3 0.6 copy.16
  (2 shorter events, 0.0 us)
Async XLA Ops:
  0.6 0.7 copy-start.1
  0.6 0.7 copy-start.2
  97.6 1.8 %copy-start = (bf16[2,16,768]{2,1,0:T(8,128)(2,1)S(1)}, bf16[2,16,768]{2,1,0:T(8,128)(2,1)}, u32[]{:S(2)}) copy-start(bf16[2,16,768]{2,1,0:T(8,128)(2,1)} %get-tuple-element.11) | copy-start | bytes 147460

commit v5 on v4

--- a/solution.py
+++ b/solution.py
@@ -17,8 +17,8 @@
     "c3", "x", "o", "y", "x", "o", "y", "a3", "xs", "o", "o", "ys", "oz", "o", "o", "o",
 )
 Y_PIECES = 2
+Y_COLS = 384
 X_PIECES = 2
-BACK = "abc"
 CORES = 2
 
 
@@ -286,28 +286,28 @@
 class Weights:
     def __init__(self, here, copies, rows_ref, wy, wz):
         self.here, self.copies = here, copies
-        self.half = rows_ref.shape[1] // 2
-        self.src_y = rows_ref.at[:, pl.ds(0, self.half)]
-        self.src_z = rows_ref.at[:, pl.ds(self.half, self.half)]
+        self.cut = Y_COLS
+        self.src_y = rows_ref.at[:, pl.ds(0, self.cut)]
+        self.src_z = rows_ref.at[:, pl.ds(self.cut, rows_ref.shape[1] - self.cut)]
         self.rows_ref, self.wy, self.wz = rows_ref, wy, wz
 
     def start_y(self):
         here = self.here
-        self.from_z = self.copies.group(self.wz.at[0, 0, pl.ds(0, here.zs - 1)])
+        self.from_z = self.copies.group(self.wy.at[pl.ds(0, here.zs - 1), 0, 0])
         self.from_z.everywhere = False
 
         @pl.when(here.z == here.n)
         def _():
             for s in outward(here.zs):
                 self.from_z.start(self.src_y, self.wy.at[here.n, here.c, here.x], here.ring("z", s))
-            self.wy[here.n, here.c, here.x] = self.rows_ref[:, :self.half]
+            self.wy[here.n, here.c, here.x] = self.rows_ref[:, :self.cut]
 
     def start_z(self):
         here = self.here
         self.along_z = self.copies.group(self.wz.at[0, 0, pl.ds(0, here.zs - 1)])
         for s in outward(here.zs):
             self.along_z.start(self.src_z, self.wz.at[here.c, here.x, here.z], here.ring("z", s))
-        self.wz[here.c, here.x, here.z] = self.rows_ref[:, self.half:]
+        self.wz[here.c, here.x, here.z] = self.rows_ref[:, self.cut:]
 
     def second_y(self):
         here = self.here
@@ -355,7 +355,7 @@
             self.copies, here.xs, here.x, lambda p: here.at(x=p), piece, X_PIECES, landed
         )
 
-    def order(self, order, z, block, part, w):
+    def order(self, order, z, block, cols, w):
         here = self.here
         mats = w.shape[0]
         owners = order.shape[0] // self.rows_ref.shape[0]
@@ -366,17 +366,17 @@
             at = z * (here.xs * CORES // owners) + q
             rows = pl.ds(pl.multiple_of(at * count, count), count)
             for i in range(mats):
-                w[i, rows, part * self.half:(part + 1) * self.half] = ordered[i * count:(i + 1) * count]
+                w[i, rows, cols] = ordered[i * count:(i + 1) * count]
 
     def order_y(self, order, w):
         p, passed = self.landed_y.pop(0)
         passed.wait_recv()
-        self.order(order[...], p, lambda x, c: self.wy[p, c, x], 0, w)
+        self.order(order[...], p, lambda x, c: self.wy[p, c, x], pl.ds(0, self.cut), w)
 
     def order_z(self, order, w):
         self.passed_z.wait_recv()
         for z in range(self.here.zs):
-            self.order(order[...], z, lambda x, c: self.wz[c, x, z], 1, w)
+            self.order(order[...], z, lambda x, c: self.wz[c, x, z], pl.ds(self.cut, w.shape[2] - self.cut), w)
 
     def finish(self):
         @pl.when(self.here.z == self.here.n)
@@ -402,7 +402,7 @@
 
 
 def pair_pass(
-    x_ref, w, sums_ref, scale_ref, cot_ref, dec_ref, vg_ref, q_s, k_s, v_s, ag_s, att_s, qg_s, kg_s, vgr_s
+    x_ref, w, sums_ref, scale_ref, cot_ref, vg_ref, q_s, k_s, v_s, ag_s, att_s, qg_s, kg_s, vgr_s
 ):
     sides, tokens, cols = x_ref.shape
     heads = scale_ref.shape[0]
@@ -472,8 +472,6 @@
         qg_s[:, cb] = ((q_back - q_unit * head_mean(q_back * q_unit)) * q_inv).astype(BF16)
         kg_s[:, cb] = ((k_back - k_unit * head_mean(k_back * k_unit)) * k_inv).astype(BF16)
 
-    decoded = (views_f + dot(att_s[...], w[3])).astype(BF16)
-    dec_ref[...] = decoded.reshape(sides, tokens, cols)
     view_term = cot.astype(F32) + dot_t(qg_s[...], w[0])
     norm_grad = dot_t(kg_s[...], w[1]) + dot_t(vgr_s[...], w[2])
     context_term = (
@@ -551,18 +549,19 @@
         part.back[0] = jnp.zeros(part.back.shape[1:], BF16)
         part.wait()
 
-    pair_pass(x_s, w, sums_s, scale_ref, cot_ref, dec_s, vg_s, *math)
+    pair_pass(x_s, w, sums_s, scale_ref, cot_ref, vg_s, *math)
+
+    for part in parts:
+        part.scatter_first(vg_s, rows)
+    decoded = x_s[...].reshape(2 * narrow * rows, cols).astype(F32) + dot(math[4][...], w[3])
+    dec_s[...] = decoded.astype(BF16).reshape(dec_s.shape)
     save = pltpu.make_async_copy(dec_s, dec_ref, local.at[3])
     save.start()
-
-    back = [parts["abc".index(name)] for name in BACK]
-    for part in back:
-        part.scatter_first(vg_s, rows)
-    for part in back:
+    for part in parts:
         part.scatter_second()
-    for part in parts:
+    for part in (b1, b2, a):
         part.scatter_third()
-    for part in parts:
+    for part in (b1, b2, a):
         part.scatter_end(out_ref)
     assert len(copies.groups) == send.shape[0]
     copies.finish()
@@ -594,8 +593,8 @@
         pltpu.VMEM(order.shape, BF16),
         pltpu.VMEM(sums.shape, BF16),
         pltpu.VMEM((wrows, cols), BF16),
-        pltpu.VMEM((narrow, CORES, xs, wrows, cols // 2), BF16),
-        pltpu.VMEM((CORES, xs, zs, wrows, cols // 2), BF16),
+        pltpu.VMEM((narrow, CORES, xs, wrows, Y_COLS), BF16),
+        pltpu.VMEM((CORES, xs, zs, wrows, cols - Y_COLS), BF16),
         pltpu.VMEM((views, rows, cols), BF16),
         pltpu.VMEM(side, BF16),
         pltpu.VMEM(side, BF16),

time: 100 us -> 98.8 us (0.988)
  Pallas kernels: 94.5 us -> 93.2 us
    pallas_call x1, Pallas kernels: 94.5 us -> 93.2 us  [whole_call(): pl.pallas_call(functools.partial(whole_kernel, wide, narrow, chunks), out...]
where the time goes in v5:
time: 98.8 us; the launch traced here: 98.6 us
  Pallas kernels  93.2 us (94%)
  local copies, waits for them, and re-layouts  3.35 us (3%)
  other arithmetic  1.38 us (1%)
    pallas_call x1, Pallas kernels, whole_call(): pl.pallas_call(functools.partial(whole_kernel, wide, narrow, chunks), out...  93.2 us
    unnamed x8, local copies, waits for them, and re-layouts  3.07 us

profile of v5, /device:TPU:1, one launch (start us, length us, event | category | flops | bytes accessed | tf_op | source)
XLA Modules:
  0.0 98.6 jit_solution(5909163353196887680)
XLA Ops:
  0.6 0.0 copy-start.1
  0.6 0.0 copy-start.2
  0.7 0.7 copy-done.1
  1.3 0.0 copy-done.2
  1.3 0.4 select_reduce_fusion.1
  1.7 0.2 copy.12
  1.9 0.1 broadcast_in_dim_reshape.4
  2.0 1.0 select_reduce_fusion.table_ref
  3.0 93.2 %whole.1 = (bf16[2,128,768]{2,1,0:T(8,128)(2,1)}, bf16[2,16,768]{2,1,0:T(8,128)(2,1)}) custom-call(bf16[2,16,768]{2,1,0:T(8,128)(2,1)} %enc_ref.1, bf16[12,4,768]{2,1,0:T(4,128)(2,1)} %bitcast.6, s32[128]{0:T(128)} %slot_ref.1, s32[2,512]{1,0:T(2,128)} %bitcast.7, s32[64,64]{1,0:T(8,128)} %select_reduce_fusion.table_ref, ...), custom_call_target="tpu_custom_call" | custom-call | tf_op jit(solution)/shard_map/whole/pallas_call | solution.py:608
  96.2 0.0 copy-start
  96.2 1.8 %copy.15 = bf16[1,2,128,768]{3,2,1,0:T(8,128)(2,1)} copy(bf16[1,2,128,768]{3,2,1,0:T(8,128)(2,1)} %bitcast.4) | data formatting | bytes 786432
  97.9 0.0 copy-done
  97.9 0.6 copy.16
  (2 shorter events, 0.0 us)
Async XLA Ops:
  0.6 0.7 copy-start.1
  0.6 0.7 copy-start.2
  96.2 1.8 %copy-start = (bf16[2,16,768]{2,1,0:T(8,128)(2,1)S(1)}, bf16[2,16,768]{2,1,0:T(8,128)(2,1)}, u32[]{:S(2)}) copy-start(bf16[2,16,768]{2,1,0:T(8,128)(2,1)} %get-tuple-element.11) | copy-start | bytes 147460

commit v6 on v5

--- a/solution.py
+++ b/solution.py
@@ -13,7 +13,7 @@
 F32 = jnp.float32
 X_SIZE = 4
 SCHEDULE = (
-    "wy", "a1", "b1", "c1", "wz", "a2", "wyx", "b2", "y", "c2", "y", "y", "b3", "x", "o", "y", "y",
+    "wy", "a1", "b1", "c1", "wz", "wyx", "a2", "y", "b2", "c2", "y", "y", "b3", "x", "o", "y", "y",
     "c3", "x", "o", "y", "x", "o", "y", "a3", "xs", "o", "o", "ys", "oz", "o", "o", "o",
 )
 Y_PIECES = 2

time: 98.8 us -> 99 us (level)
  no operation moved by 1% of the time
where the time goes in v6:
time: 99 us; the launch traced here: 98.8 us
  Pallas kernels  93.4 us (94%)
  local copies, waits for them, and re-layouts  3.35 us (3%)
  other arithmetic  1.38 us (1%)
    pallas_call x1, Pallas kernels, whole_call(): pl.pallas_call(functools.partial(whole_kernel, wide, narrow, chunks), out...  93.4 us
    unnamed x8, local copies, waits for them, and re-layouts  3.07 us

profile of v6, /device:TPU:1, one launch (start us, length us, event | category | flops | bytes accessed | tf_op | source)
XLA Modules:
  0.0 98.8 jit_solution(15892039365027174019)
XLA Ops:
  0.6 0.0 copy-start.1
  0.6 0.0 copy-start.2
  0.7 0.7 copy-done.1
  1.3 0.0 copy-done.2
  1.3 0.4 select_reduce_fusion.1
  1.7 0.2 copy.12
  1.9 0.1 broadcast_in_dim_reshape.4
  2.0 1.0 select_reduce_fusion.table_ref
  3.0 93.4 %whole.1 = (bf16[2,128,768]{2,1,0:T(8,128)(2,1)}, bf16[2,16,768]{2,1,0:T(8,128)(2,1)}) custom-call(bf16[2,16,768]{2,1,0:T(8,128)(2,1)} %enc_ref.1, bf16[12,4,768]{2,1,0:T(4,128)(2,1)} %bitcast.6, s32[128]{0:T(128)} %slot_ref.1, s32[2,512]{1,0:T(2,128)} %bitcast.7, s32[64,64]{1,0:T(8,128)} %select_reduce_fusion.table_ref, ...), custom_call_target="tpu_custom_call" | custom-call | tf_op jit(solution)/shard_map/whole/pallas_call | solution.py:608
  96.4 0.0 copy-start
  96.4 1.8 %copy.15 = bf16[1,2,128,768]{3,2,1,0:T(8,128)(2,1)} copy(bf16[1,2,128,768]{3,2,1,0:T(8,128)(2,1)} %bitcast.4) | data formatting | bytes 786432
  98.2 0.0 copy-done
  98.2 0.6 copy.16
  (2 shorter events, 0.0 us)
Async XLA Ops:
  0.6 0.7 copy-start.1
  0.6 0.7 copy-start.2
  96.4 1.8 %copy-start = (bf16[2,16,768]{2,1,0:T(8,128)(2,1)S(1)}, bf16[2,16,768]{2,1,0:T(8,128)(2,1)}, u32[]{:S(2)}) copy-start(bf16[2,16,768]{2,1,0:T(8,128)(2,1)} %get-tuple-element.11) | copy-start | bytes 147460
